TPU v7x, 32 devices: a whole 2x2x4 slice. The times are simulated.
32 devices in a mesh: dp: 4 (over z), ctx: 2 (over x), fsdp: 4 (over y, core).
Axes of the slice: x: 2, y: 2, z: 4, core: 2. Of those that a mesh axis runs over, the one named last changes fastest.
Arguments:
- hidden_in: bfloat16 [4, 1024, 2304], P('dp', ('ctx', 'fsdp')), may hold values from -6 to 6
- positions: int32 [4, 1024], P('dp', ('ctx', 'fsdp')), may hold values from 0 to 5118, as said below
- cotangent: bfloat16 [4, 1024, 2304], P('dp', ('ctx', 'fsdp')), may hold values from -6 to 6
- w_qkv: bfloat16 [2304, 4096], P(('dp', 'ctx', 'fsdp')), may hold values from -0.1875 to 0.1875
- w_out: bfloat16 [2048, 2304], P(('dp', 'ctx', 'fsdp')), may hold values from -0.125 to 0.125
- w_gate_up: bfloat16 [2304, 18432], P(('dp', 'ctx', 'fsdp')), may hold values from -0.125 to 0.125
- w_down: bfloat16 [9216, 2304], P(('dp', 'ctx', 'fsdp')), may hold values from -0.0625 to 0.0625
- gains: bfloat16 [4, 2304], P(None, ('dp', 'ctx', 'fsdp')), may hold values from -0.5 to 0.5
- m_qkv: float32 [2304, 4096], P(('dp', 'ctx', 'fsdp')), may hold values from -64.128 to 64.128
- v_qkv: float32 [2304, 4096], P(('dp', 'ctx', 'fsdp')), may hold values from 241.664 to 3878.912
- m_out: float32 [2048, 2304], P(('dp', 'ctx', 'fsdp')), may hold values from -64.128 to 64.128
- v_out: float32 [2048, 2304], P(('dp', 'ctx', 'fsdp')), may hold values from 241.664 to 3878.912
- m_gate_up: float32 [2304, 18432], P(('dp', 'ctx', 'fsdp')), may hold values from -21.312 to 21.312
- v_gate_up: float32 [2304, 18432], P(('dp', 'ctx', 'fsdp')), may hold values from 26.9312 to 431.104
- m_down: float32 [9216, 2304], P(('dp', 'ctx', 'fsdp')), may hold values from -42.624 to 42.624
- v_down: float32 [9216, 2304], P(('dp', 'ctx', 'fsdp')), may hold values from 107.7248 to 1724.416
- m_gains: float32 [4, 2304], P(None, ('dp', 'ctx', 'fsdp')), may hold values from -64.128 to 64.128
- v_gains: float32 [4, 2304], P(None, ('dp', 'ctx', 'fsdp')), may hold values from 241.664 to 3878.912
Outputs:
- block_out: bfloat16 [4, 1024, 2304], P('dp', ('ctx', 'fsdp'))
- input_grad: float32 [4, 1024, 2304], P('dp', ('ctx', 'fsdp'))
- new_qkv: float32 [2304, 4096], P(('dp', 'ctx', 'fsdp'))
- new_m_qkv: float32 [2304, 4096], P(('dp', 'ctx', 'fsdp'))
- new_v_qkv: float32 [2304, 4096], P(('dp', 'ctx', 'fsdp'))
- new_out: float32 [2048, 2304], P(('dp', 'ctx', 'fsdp'))
- new_m_out: float32 [2048, 2304], P(('dp', 'ctx', 'fsdp'))
- new_v_out: float32 [2048, 2304], P(('dp', 'ctx', 'fsdp'))
- new_gate_up: float32 [2304, 18432], P(('dp', 'ctx', 'fsdp'))
- new_m_gate_up: float32 [2304, 18432], P(('dp', 'ctx', 'fsdp'))
- new_v_gate_up: float32 [2304, 18432], P(('dp', 'ctx', 'fsdp'))
- new_down: float32 [9216, 2304], P(('dp', 'ctx', 'fsdp'))
- new_m_down: float32 [9216, 2304], P(('dp', 'ctx', 'fsdp'))
- new_v_down: float32 [9216, 2304], P(('dp', 'ctx', 'fsdp'))
- new_gains: float32 [4, 2304], P(None, ('dp', 'ctx', 'fsdp'))
- new_m_gains: float32 [4, 2304], P(None, ('dp', 'ctx', 'fsdp'))
- new_v_gains: float32 [4, 2304], P(None, ('dp', 'ctx', 'fsdp'))
Inputs may be any that keep to these rules, and one draw needn't show every extreme that they name: In each sequence the stored tokens fall into 4 aligned blocks of 256 slots holding rising consecutive positions; the blocks start at p0, p0 + 256, ..., p0 + 768 for one p0 of 0 to 4095 per sequence, one sequence having p0 = 0 and another p0 = 4095; the two blocks stored at slots 2c and 2c + 1 are the blocks numbered b and 3 - b in either order.
All inputs are finite; a program needn't handle non-finite values.
Results may differ from a plain program's by a relative error of at most 0.018.
Values may be sent and summed in bfloat16 or wider, within the bound.
No kernel may reach another device: no remote copies, remote signals or barrier semaphores. Data moves between devices by JAX's collectives and lax.ppermute only.
A program may use at most 960 MiB of HBM per device.

v0:
```python
import jax
import jax.numpy as jnp
from jax import lax
from jax.sharding import Mesh, PartitionSpec as P

HEADS = 8
KV_HEADS = 4
HEAD_DIM = 256
STEP = 10

NORM_EPS = 1e-06
SOFT_CAP = 50.0
THETA = 10000.0
BETA_ONE = 0.9
BETA_TWO = 0.95
ADAM_EPS = 1e-08
MATRIX_RATE = 0.03
GAIN_RATE = 0.2
WEIGHT_DECAY = 0.1

DP = ("dh", "dl")
PLANE = ("ctx", "fy", "core")
ALL = DP + PLANE
LADDER = DP + ("ctx",)
GROUP = PLANE
ACROSS = DP


def f32(v):
    return v.astype(jnp.float32)


def bf(v):
    return v.astype(jnp.bfloat16)


def dot(left, right, dims):
    return lax.dot_general(left, right, (dims, ((), ())), preferred_element_type=jnp.float32)


def mm(left, right):
    return dot(left, right, ((1,), (0,)))


def mm_nt(left, right):
    return dot(left, right, ((1,), (1,)))


def mm_tn(left, right):
    return dot(left, right, ((0,), (0,)))


def rms_scale(values, gain):
    inverse = lax.rsqrt(jnp.mean(values * values, axis=-1, keepdims=True) + NORM_EPS)
    return values * inverse * (1.0 + gain)


def rotary_tables(places):
    half = HEAD_DIM // 2
    freqs = THETA ** (-(jnp.arange(half, dtype=jnp.float32) * 2.0 / HEAD_DIM))
    angles = f32(places)[:, None] * freqs[None, :]
    return (jnp.cos(angles), jnp.sin(angles))


def rotary(values, cosine, sine):
    half = HEAD_DIM // 2
    first = values[..., :half]
    second = values[..., half:]
    return jnp.concatenate(
        [first * cosine - second * sine, second * cosine + first * sine], axis=-1
    )


def unrotary(values, cosine, sine):
    return rotary(values, cosine, -sine)


def adam_step(weight, grad, first, second, rate, decay):
    first_new = BETA_ONE * first + (1.0 - BETA_ONE) * grad
    second_new = BETA_TWO * second + (1.0 - BETA_TWO) * grad * grad
    ratio = (
        first_new
        / (1.0 - BETA_ONE**STEP)
        / (jnp.sqrt(second_new / (1.0 - BETA_TWO**STEP)) + ADAM_EPS)
    )
    return (weight - rate * (ratio + decay * weight), first_new, second_new)


def gather(v, axes, axis=0):
    return lax.all_gather(v, axes, axis=axis, tiled=True)


def scatter_sum(v, axes):
    return lax.psum_scatter(v, axes, scatter_dimension=0, tiled=True)


def swap(v, axes):
    return lax.all_to_all(v, axes, split_axis=0, concat_axis=0, tiled=True)


def hold(v):
    return lax.optimization_barrier(v)


def flip(v, axis):
    return lax.ppermute(v, axis, [(0, 1), (1, 0)])


def plane_gather(own):
    me = lax.axis_index(PLANE)
    over_y = flip(own, "fy")
    over_x = flip(own, "ctx")
    blocks = [own, over_y, over_x, flip(over_y, "ctx")]
    whole = jnp.zeros((8,) + own.shape, own.dtype)
    for bits, block in enumerate(blocks):
        whole = lax.dynamic_update_index_in_dim(whole, block, me ^ (2 * bits), 0)
        whole = lax.dynamic_update_index_in_dim(whole, flip(block, "core"), me ^ (2 * bits + 1), 0)
    return whole.reshape((-1,) + own.shape[1:])


def plane_scatter(parts):
    size = parts.shape[0] // 8
    half = size // 2
    col, row, core = (lax.axis_index(axis) for axis in PLANE)
    parts = parts.reshape((4, 2, size) + parts.shape[1:])
    sent = lax.dynamic_index_in_dim(parts, 1 - core, 1, keepdims=False)
    kept = lax.dynamic_index_in_dim(parts, core, 1, keepdims=False)
    both = bf(f32(kept) + f32(flip(sent, "core")))
    own, over_y, over_x, corner = (
        lax.dynamic_index_in_dim(both, (2 * col + row) ^ bits, 0, keepdims=False) for bits in range(4)
    )
    got_y = flip(corner[:half], "ctx")
    got_x = flip(corner[half:], "fy")
    over_y = jnp.concatenate([bf(f32(over_y[:half]) + f32(got_y)), over_y[half:]], axis=0)
    over_x = jnp.concatenate([over_x[:half], bf(f32(over_x[half:]) + f32(got_x))], axis=0)
    return f32(own) + f32(flip(over_x, "ctx")) + f32(flip(over_y, "fy"))


def line_gather(own):
    count = lax.axis_size(DP)
    row = [own]
    up, down = (own, own)
    for step in range(1, count):
        up = lax.ppermute(up, DP, [(i, i + 1) for i in range(step - 1, count - 1)])
        down = lax.ppermute(down, DP, [(i + 1, i) for i in range(count - step)])
        row = [up] + row + [down]
    return lax.dynamic_slice_in_dim(jnp.stack(row), count - 1 - lax.axis_index(DP), count, axis=0)


def ring_pairs():
    count = lax.axis_size(DP)
    ring = [2 * z for z in range(count)] + [2 * z + 1 for z in reversed(range(count))]
    onward = [(ring[i], ring[(i + 1) % len(ring)]) for i in range(len(ring))]
    return onward, [(b, a) for a, b in onward]


def ring_gather(own):
    onward, back = ring_pairs()
    half = own.shape[0] // 2
    steps = [[own]]
    behind, ahead = (own, own)
    for _ in range(len(onward) // 2 - 1):
        behind = lax.ppermute(behind, LADDER, onward)
        ahead = lax.ppermute(ahead, LADDER, back)
        steps.append([behind, ahead])
    steps.append(
        [
            lax.ppermute(behind[:half], LADDER, onward),
            lax.ppermute(ahead[half:], LADDER, back),
        ]
    )
    return steps


def two_parts(steps):
    return [
        jnp.concatenate(sum(steps[:3], []), axis=0),
        jnp.concatenate(sum(steps[3:], []), axis=0),
    ]


def steps_of(parts, size):
    early, late = parts
    steps = [early[:size], early[size : 3 * size], early[3 * size :]]
    return steps + [late[: 2 * size], late[2 * size :]]


def ring_scatter(pieces):
    onward, back = ring_pairs()
    size = pieces[0].shape[0]
    half = size // 2
    ahead = lax.ppermute(pieces[-1][:half], LADDER, onward)
    behind = lax.ppermute(pieces[-1][half:], LADDER, back)
    for step in range(len(pieces) - 2, 0, -1):
        to_behind, to_ahead = (pieces[step][:size], pieces[step][size:])
        if step == len(pieces) - 2:
            to_ahead = jnp.concatenate(
                [bf(f32(to_ahead[:half]) + f32(ahead)), to_ahead[half:]], axis=0
            )
            to_behind = jnp.concatenate(
                [to_behind[:half], bf(f32(to_behind[half:]) + f32(behind))], axis=0
            )
        else:
            to_ahead = bf(f32(to_ahead) + f32(ahead))
            to_behind = bf(f32(to_behind) + f32(behind))
        to_ahead, to_behind = hold((to_ahead, to_behind))
        ahead = lax.ppermute(to_ahead, LADDER, onward)
        behind = lax.ppermute(to_behind, LADDER, back)
    return f32(pieces[0]) + f32(ahead) + f32(behind)


def quad_blocks(own, late=None):
    over_y = flip(own, "fy")
    if late is not None:
        over_y, _ = hold((over_y, late))
    return [own, flip(own, "core"), over_y, flip(over_y, "core")]


def quad_place(blocks, parts):
    me = lax.axis_index(("fy", "core"))
    count, rows, cols = blocks[0][0].shape
    whole = jnp.zeros((count, 4, rows, parts * cols), blocks[0][0].dtype)
    for part in range(parts):
        for bits, block in enumerate(blocks[part]):
            whole = lax.dynamic_update_slice(
                whole, block[:, None], (0, me ^ bits, 0, part * cols)
            )
    return whole


def core_sum(parts, late):
    core = lax.axis_index("core")
    parts = parts.reshape(parts.shape[:1] + (2, 2) + parts.shape[2:])
    sent = lax.dynamic_index_in_dim(parts, 1 - core, 2, keepdims=False)
    kept = lax.dynamic_index_in_dim(parts, core, 2, keepdims=False)
    kept, got, _ = hold((kept, flip(sent, "core"), late))
    return bf(f32(kept) + f32(got))


def row_sum(both, late=()):
    row = lax.axis_index("fy")
    sent = lax.dynamic_index_in_dim(both, 1 - row, 1, keepdims=False)
    kept = lax.dynamic_index_in_dim(both, row, 1, keepdims=False)
    kept, got, _ = hold((kept, flip(sent, "fy"), late))
    return bf(f32(kept) + f32(got))


def ladder_shards(
    hidden_in,
    positions,
    cotangent,
    w_qkv,
    w_out,
    w_gate_up,
    w_down,
    gains,
    m_qkv,
    v_qkv,
    m_out,
    v_out,
    m_gate_up,
    v_gate_up,
    m_down,
    v_down,
    m_gains,
    v_gains,
):
    x_own = hidden_in[0]
    tok, width = x_own.shape
    rows = w_qkv.shape[0]
    planes = lax.axis_size(DP)
    group = lax.axis_size(LADDER)
    q_width = HEADS * HEAD_DIM
    core = lax.axis_index("core")

    q_cols = w_qkv[:, :q_width].reshape(rows, HEADS, HEAD_DIM)
    kv_cols = w_qkv[:, q_width:].reshape(rows, 2, KV_HEADS, HEAD_DIM)
    kv_cols = jnp.swapaxes(kv_cols, 1, 2).reshape(rows, HEADS, HEAD_DIM)
    pieces = jnp.swapaxes(jnp.concatenate([q_cols, kv_cols], axis=2), 0, 1)
    first = jnp.stack([positions[0, 0] // 128, positions[0, 0] % 128])
    own_gains = jnp.concatenate([gains.reshape(4 * rows), bf(first)])[None, None]
    own_gains = jnp.pad(own_gains, ((0, 0), (0, 7), (0, 2 * HEAD_DIM - 4 * rows - 2)))
    pieces = jnp.concatenate(
        [pieces, jnp.broadcast_to(own_gains, (HEADS,) + own_gains.shape[1:])], axis=1
    )
    got = swap(pieces, PLANE)
    got, x_sent, out_line = hold((got, x_own, w_out))
    x_all = plane_gather(x_sent)
    out_line = line_gather(out_line)
    first = got[:, rows, 4 * rows : 4 * rows + 2].astype(jnp.int32)
    pos_all = first[:, :1] * 128 + first[:, 1:] + jnp.arange(tok, dtype=jnp.int32)[None]
    pos_all = pos_all.reshape(-1)
    cosine, sine = rotary_tables(pos_all)
    got = lax.all_gather(got, DP)
    ff_own = w_down.shape[0] * 4
    cols = []
    for part in range(2):
        piece = w_gate_up[:, part * group * ff_own : (part + 1) * group * ff_own]
        cols.append(jnp.swapaxes(piece.reshape(rows, group, ff_own), 0, 1))
    got, cols[0], w_down_late = hold((got, cols[0], w_down))
    w_own = got[:, :, :rows].reshape(width, 2 * HEAD_DIM)
    gain_vals = got[:, :, rows, : 4 * rows].reshape(planes * HEADS, 4, rows)
    gain_vals = f32(jnp.swapaxes(gain_vals, 0, 1).reshape(4, width))
    out_full = lax.all_gather(out_line, PLANE, axis=1, tiled=False).reshape(q_width, width)
    cols[0] = swap(cols[0], LADDER)

    normed_all = hold(bf(rms_scale(f32(x_all), gain_vals[0])))
    qkv = mm(normed_all, w_own)
    query = bf(rotary(qkv[:, :HEAD_DIM], cosine, sine) * HEAD_DIM ** (-0.5))
    half = qkv[:, HEAD_DIM:]
    mine = jnp.where(core == 0, bf(rotary(half, cosine, sine)), bf(half))
    other = flip(mine, "core")
    key = jnp.where(core == 0, mine, other)
    value = jnp.where(core == 0, other, mine)
    scores = mm_nt(query, key)
    capped = SOFT_CAP * jnp.tanh(scores / SOFT_CAP)
    weights = jnp.where(pos_all[:, None] >= pos_all[None, :], jnp.exp(capped), 0.0)
    weights_b = bf(weights)
    total = jnp.sum(weights, axis=-1, keepdims=True)
    attn = mm(weights_b, value) / total
    cols[0], attn_sent = hold((cols[0], bf(attn)))
    attn_own = swap(attn_sent.reshape(HEADS, tok, HEAD_DIM), PLANE)
    cols[0], cols[1], _ = hold((cols[0], cols[1], attn_own))
    cols[1] = swap(cols[1], LADDER)
    attn_own = jnp.swapaxes(attn_own, 0, 1).reshape(tok, q_width)
    mixed = mm(attn_own, out_full)

    x_rows = f32(x_own)
    branch_one, pull_one = jax.vjp(rms_scale, mixed, gain_vals[1])
    resid = x_rows + branch_one
    normed_two, pull_two = jax.vjp(rms_scale, resid, gain_vals[2])

    tokens_own = bf(normed_two)
    steps = ring_gather(tokens_own)
    cols[1], _ = hold((cols[1], tokens_own))
    down_own = quad_place([quad_blocks(w_down_late[None], tokens_own)], 1).reshape(ff_own, width)
    gate_up_own = [quad_blocks(cols[0], tokens_own), quad_blocks(cols[1])]
    gate_up_own = quad_place(gate_up_own, 2).reshape(width, 2 * ff_own)
    tokens = jnp.concatenate(sum(steps, []), axis=0)
    gate_up = mm(tokens, gate_up_own)

    def gated(gate, up_part):
        return jax.nn.gelu(gate, approximate=True) * up_part

    inner = bf(gated(gate_up[:, :ff_own], gate_up[:, ff_own:]))
    late = tokens.shape[0] - 3 * tok
    down = bf(mm(inner, down_own))
    attn_cols = attn_own.reshape(tok, planes, HEADS, w_out.shape[0])
    attn_cols = jnp.transpose(attn_cols, (2, 0, 1, 3)).reshape(HEADS, tok, HEAD_DIM)
    attn_cols, down = hold((attn_cols, down))
    attn_cols = swap(attn_cols, PLANE).reshape(HEADS * tok, HEAD_DIM)
    down = ring_scatter(steps_of((down[:late], down[late:]), tok))
    down, attn_cols = hold((down, attn_cols))
    branch_two, pull_three = jax.vjp(rms_scale, down, gain_vals[3])
    block_out = bf(resid + branch_two)[None]
    grad_top = f32(cotangent[0])
    grad_down_in, gain_grad_three = pull_three(grad_top)
    steps = ring_gather(bf(grad_down_in))
    grad_downs = two_parts(steps)
    grad_gus, parts = ([], [])
    for piece, kept in zip(grad_downs, (gate_up[:late], gate_up[late:])):
        _, pull = jax.vjp(gated, kept[:, :ff_own], kept[:, ff_own:])
        grad_gus.append(bf(jnp.concatenate(pull(mm_nt(piece, down_own)), axis=1)))
        grad_gu, _ = hold((grad_gus[-1], steps[3][0]))
        parts.append(bf(mm_nt(grad_gu, gate_up_own)))
    tokens, inner, grad_downs, grad_gus, parts = hold(
        (tokens, inner, grad_downs, grad_gus, parts)
    )
    grad_normed_two = ring_scatter(steps_of(parts, tok))
    grad_gu_b = jnp.concatenate(grad_gus, axis=0)
    grad_halves = [bf(mm_tn(tokens, grad_gu_b[:, :ff_own])), bf(mm_tn(tokens, grad_gu_b[:, ff_own:]))]
    grad_down_w = bf(mm_tn(inner, jnp.concatenate(grad_downs, axis=0)))
    grad_normed_two, _, _ = hold((grad_normed_two, grad_halves, grad_down_w))
    grad_resid_two, _ = pull_two(grad_normed_two)
    grad_resid = grad_top + grad_resid_two
    grad_mixed, gain_grad_one = pull_one(grad_resid)
    grad_mixed_b = bf(grad_mixed)

    grad_attn = bf(mm_nt(grad_mixed_b, out_full)).reshape(tok, HEADS, HEAD_DIM)
    grad_head = swap(jnp.swapaxes(grad_attn, 0, 1), PLANE).reshape(HEADS * tok, HEAD_DIM)
    grad_head = f32(grad_head)
    rho = bf(grad_head / total)
    delta = jnp.sum(grad_head * attn, axis=-1, keepdims=True) / total
    pulled = mm_nt(rho, value)
    grad_scores = bf((pulled - delta) * weights * (1.0 - (capped / SOFT_CAP) ** 2))
    grad_query = mm(grad_scores, key) * HEAD_DIM ** (-0.5)
    grad_key = mm_tn(grad_scores, query)
    grad_value = mm_tn(weights_b, rho)
    sent = jnp.where(core == 0, grad_value, grad_key)
    grad_half = jnp.where(core == 0, grad_key, grad_value) + flip(sent, "core")
    grad_half = jnp.where(core == 0, unrotary(grad_half, cosine, sine), grad_half)
    grad_qkv = bf(jnp.concatenate([unrotary(grad_query, cosine, sine), grad_half], axis=1))
    others = bf(jnp.stack([gain_grad_one, gain_grad_three]))
    others = jnp.concatenate([grad_mixed_b, jnp.pad(others, ((0, 14), (0, 0)))], axis=0)
    others = lax.all_gather(others, PLANE)
    grad_qkv, others = hold((grad_qkv, others))
    grad_mixed_all = others[:, :tok].reshape(HEADS * tok, width)
    others = jnp.sum(f32(others[:, tok : tok + 2]), axis=0).reshape(2, planes, HEADS, rows)
    others = lax.dynamic_index_in_dim(others, lax.axis_index(PLANE), 2, keepdims=False)
    others = jnp.swapaxes(others, 0, 1).reshape(planes, 1, 2 * rows)
    others = bf(jnp.pad(others, ((0, 0), (0, 7), (0, 2 * HEAD_DIM - 2 * rows))))
    grad_w = bf(mm_tn(normed_all, grad_qkv))
    grad_qkv, grad_w = hold((grad_qkv, grad_w))
    sums = [core_sum(v.reshape(group, 4, rows, ff_own), grad_qkv) for v in grad_halves]
    sums.append(core_sum(grad_down_w.reshape(1, 4, ff_own // 4, width), grad_qkv))
    grad_w = grad_w.reshape(planes, -1, 2 * HEAD_DIM)
    grad_out_w = bf(mm_tn(attn_cols, grad_mixed_all)).reshape(planes, -1, 2 * HEAD_DIM)
    grad_w = jnp.concatenate([grad_w, grad_out_w, others], axis=1)
    grad_w, grad_qkv = hold((grad_w, grad_qkv))
    grad_normed = plane_scatter(bf(mm_nt(grad_qkv, w_own)))
    grad_w = scatter_sum(grad_w, DP)[0]
    grad_halves = [swap(row_sum(sums[0]), LADDER)]
    grad_halves.append(row_sum(sums[1], grad_halves[0]))
    grad_down_w, grad_halves[1] = hold((sums[2], grad_halves[1]))
    grad_down_w = f32(row_sum(grad_down_w)[0])
    others = f32(grad_w[-8, : 2 * rows]).reshape(2, rows)
    grad_out_w = f32(grad_w[HEADS * rows : -8].reshape(w_out.shape))
    grad_w = grad_w[: HEADS * rows].reshape(HEADS, rows, 2 * HEAD_DIM)
    grad_halves[1] = swap(grad_halves[1], LADDER)
    grad_w, grad_halves[1], grad_normed = hold((grad_w, grad_halves[1], grad_normed))
    grad_halves = [jnp.swapaxes(v, 0, 1).reshape(rows, group * ff_own) for v in grad_halves]
    grad_gate_up_w = f32(jnp.concatenate(grad_halves, axis=1))
    _, pull_zero = jax.vjp(rms_scale, x_rows, gain_vals[0])
    grad_x_zero, _ = pull_zero(grad_normed)
    input_grad = (grad_resid + grad_x_zero)[None]
    grad_w = f32(jnp.swapaxes(swap(grad_w, PLANE), 0, 1))
    grad_q_w = grad_w[:, :, :HEAD_DIM].reshape(rows, q_width)
    grad_kv_w = grad_w[:, :, HEAD_DIM:].reshape(rows, KV_HEADS, 2, HEAD_DIM)
    grad_kv_w = jnp.swapaxes(grad_kv_w, 1, 2).reshape(rows, q_width)
    grad_qkv_w = jnp.concatenate([grad_q_w, grad_kv_w], axis=1)

    gain_zero = jnp.sum(f32(w_qkv) * grad_qkv_w, axis=1) / (1.0 + f32(gains[0]))
    gain_two = jnp.sum(f32(w_gate_up) * grad_gate_up_w, axis=1) / (1.0 + f32(gains[2]))
    grad_gains = jnp.stack([gain_zero, others[0], gain_two, others[1]], axis=0)

    return (
        (block_out, input_grad)
        + adam_step(f32(w_qkv), grad_qkv_w, m_qkv, v_qkv, MATRIX_RATE, WEIGHT_DECAY)
        + adam_step(f32(w_out), grad_out_w, m_out, v_out, MATRIX_RATE, WEIGHT_DECAY)
        + adam_step(f32(w_gate_up), grad_gate_up_w, m_gate_up, v_gate_up, MATRIX_RATE, WEIGHT_DECAY)
        + adam_step(f32(w_down), grad_down_w, m_down, v_down, MATRIX_RATE, WEIGHT_DECAY)
        + adam_step(f32(gains), grad_gains, m_gains, v_gains, GAIN_RATE, 0.0)
    )


def token_attention(x_own, pos_own, w_qkv, w_out, gains):
    tok = x_own.shape[0]
    q_width = HEADS * HEAD_DIM
    k_width = KV_HEADS * HEAD_DIM
    groups = HEADS // KV_HEADS
    qkv_full = gather(w_qkv, ALL)
    out_full = gather(w_out, ALL)
    gain_vals = f32(gather(gains, ALL, 1))
    normed = bf(rms_scale(f32(x_own), gain_vals[0]))
    qkv = mm(normed, qkv_full)
    cosine, sine = rotary_tables(pos_own)
    cosine, sine = (cosine[:, None, :], sine[:, None, :])
    query = rotary(qkv[:, :q_width].reshape(tok, HEADS, HEAD_DIM), cosine, sine)
    query = bf(query * HEAD_DIM ** (-0.5)).reshape(tok, KV_HEADS, groups, HEAD_DIM)
    key_own = qkv[:, q_width : q_width + k_width].reshape(tok, KV_HEADS, HEAD_DIM)
    key = gather(bf(rotary(key_own, cosine, sine)), PLANE)
    value = gather(bf(qkv[:, q_width + k_width :]).reshape(tok, KV_HEADS, HEAD_DIM), PLANE)
    pos_all = gather(pos_own, PLANE)
    count = pos_all.shape[0]
    scores = jnp.einsum("tgjd,sgd->gjts", query, key, preferred_element_type=jnp.float32)
    capped = SOFT_CAP * jnp.tanh(scores / SOFT_CAP)
    weights = jnp.where(pos_own[:, None] >= pos_all[None, :], jnp.exp(capped), 0.0)
    weights_b = bf(weights)
    total = jnp.sum(weights, axis=-1)
    attn = jnp.einsum("gjts,sgd->gjtd", weights_b, value, preferred_element_type=jnp.float32)
    attn = attn / total[..., None]
    attn_b = bf(jnp.transpose(attn, (2, 0, 1, 3)).reshape(tok, q_width))
    mixed = mm(attn_b, out_full)

    def backward(grad_mixed_b):
        grad_attn = mm_nt(grad_mixed_b, out_full).reshape(tok, KV_HEADS, groups, HEAD_DIM)
        grad_heads = jnp.transpose(grad_attn, (1, 2, 0, 3))
        rho = bf(grad_heads / total[..., None])
        delta = jnp.sum(grad_heads * attn, axis=-1) / total
        pulled = jnp.einsum("gjtd,sgd->gjts", rho, value, preferred_element_type=jnp.float32)
        grad_scores = bf(
            (pulled - delta[..., None]) * weights * (1.0 - (capped / SOFT_CAP) ** 2)
        )
        grad_query = jnp.einsum(
            "gjts,sgd->tgjd", grad_scores, key, preferred_element_type=jnp.float32
        ).reshape(tok, HEADS, HEAD_DIM)
        grad_key = jnp.einsum(
            "gjts,tgjd->sgd", grad_scores, query, preferred_element_type=jnp.float32
        ).reshape(count, k_width)
        grad_value = jnp.einsum(
            "gjts,gjtd->sgd", weights_b, rho, preferred_element_type=jnp.float32
        ).reshape(count, k_width)
        grad_kv = scatter_sum(jnp.concatenate([grad_key, grad_value], axis=1), PLANE)
        grad_query = unrotary(grad_query * HEAD_DIM ** (-0.5), cosine, sine)
        grad_key = unrotary(grad_kv[:, :k_width].reshape(tok, KV_HEADS, HEAD_DIM), cosine, sine)
        grad_qkv = bf(
            jnp.concatenate(
                [
                    grad_query.reshape(tok, q_width),
                    grad_key.reshape(tok, k_width),
                    grad_kv[:, k_width:],
                ],
                axis=1,
            )
        )
        grad_normed = mm_nt(grad_qkv, qkv_full)
        grad_qkv_w = f32(scatter_sum(bf(mm_tn(normed, grad_qkv)), ALL))
        grad_out_w = f32(scatter_sum(bf(mm_tn(attn_b, grad_mixed_b)), ALL))
        return grad_normed, grad_qkv_w, grad_out_w

    return mixed, gain_vals, backward


def wide_shards(
    hidden_in,
    positions,
    cotangent,
    w_qkv,
    w_out,
    w_gate_up,
    w_down,
    gains,
    m_qkv,
    v_qkv,
    m_out,
    v_out,
    m_gate_up,
    v_gate_up,
    m_down,
    v_down,
    m_gains,
    v_gains,
):
    x_own = hidden_in[0]
    rows, width = (w_qkv.shape[0], x_own.shape[1])
    group, across = (lax.axis_size(GROUP), lax.axis_size(ACROSS))
    ff_piece = w_down.shape[0]
    ff_own = across * ff_piece
    gu_pieces = w_gate_up.reshape(rows, 2, across, group, ff_piece)
    gu_pieces = jnp.transpose(gu_pieces, (3, 0, 1, 2, 4)).reshape(group * rows, 2 * ff_own)

    mixed, gain_vals, attention_back = token_attention(x_own, positions[0], w_qkv, w_out, gains)
    gu_own = gather(swap(gu_pieces, GROUP), ACROSS)
    down_own = gather(w_down, ACROSS)

    x_rows = f32(x_own)
    branch_one, pull_one = jax.vjp(rms_scale, mixed, gain_vals[1])
    resid = x_rows + branch_one
    normed_two, pull_two = jax.vjp(rms_scale, resid, gain_vals[2])
    tokens_b = gather(bf(normed_two), GROUP)
    gate_up = mm(tokens_b, gu_own)
    inner, pull_gelu = jax.vjp(
        lambda gate, up_part: jax.nn.gelu(gate, approximate=True) * up_part,
        gate_up[:, :ff_own],
        gate_up[:, ff_own:],
    )
    inner_b = bf(inner)
    down = f32(scatter_sum(bf(mm(inner_b, down_own)), GROUP))
    branch_two, pull_three = jax.vjp(rms_scale, down, gain_vals[3])
    block_out = bf(resid + branch_two)[None]
    grad_top = f32(cotangent[0])
    grad_down_in, gain_grad_three = pull_three(grad_top)
    grad_down_b = gather(bf(grad_down_in), GROUP)
    grad_gate, grad_up = pull_gelu(mm_nt(grad_down_b, down_own))
    grad_gu_b = bf(jnp.concatenate([grad_gate, grad_up], axis=1))
    grad_normed_two = f32(scatter_sum(bf(mm_nt(grad_gu_b, gu_own)), GROUP))
    grad_gate_up_w = scatter_sum(bf(mm_tn(tokens_b, grad_gu_b)), ACROSS)
    grad_down_w = f32(scatter_sum(bf(mm_tn(inner_b, grad_down_b)), ACROSS))

    grad_resid_two, gain_grad_two = pull_two(grad_normed_two)
    grad_resid = grad_top + grad_resid_two
    grad_mixed, gain_grad_one = pull_one(grad_resid)
    grad_normed, grad_qkv_w, grad_out_w = attention_back(bf(grad_mixed))
    _, pull_zero = jax.vjp(rms_scale, x_rows, gain_vals[0])
    grad_x_zero, gain_grad_zero = pull_zero(grad_normed)
    input_grad = (grad_resid + grad_x_zero)[None]

    grad_gate_up_w = swap(grad_gate_up_w, GROUP).reshape(group, rows, 2, across, ff_piece)
    grad_gate_up_w = f32(jnp.transpose(grad_gate_up_w, (1, 2, 3, 0, 4)).reshape(rows, -1))
    gain_term = jnp.stack([gain_grad_zero, gain_grad_one, gain_grad_two, gain_grad_three], axis=0)
    grad_gains = lax.psum_scatter(gain_term, ALL, scatter_dimension=1, tiled=True)

    return (
        (block_out, input_grad)
        + adam_step(f32(w_qkv), grad_qkv_w, m_qkv, v_qkv, MATRIX_RATE, WEIGHT_DECAY)
        + adam_step(f32(w_out), grad_out_w, m_out, v_out, MATRIX_RATE, WEIGHT_DECAY)
        + adam_step(f32(w_gate_up), grad_gate_up_w, m_gate_up, v_gate_up, MATRIX_RATE, WEIGHT_DECAY)
        + adam_step(f32(w_down), grad_down_w, m_down, v_down, MATRIX_RATE, WEIGHT_DECAY)
        + adam_step(f32(gains), grad_gains, m_gains, v_gains, GAIN_RATE, 0.0)
    )


def solution(mesh):
    sizes = dict(mesh.shape)
    fine = Mesh(
        mesh.devices.reshape(sizes["dp"] // 2, 2, sizes["ctx"], sizes["fsdp"] // 2, 2),
        ("dh", "dl", "ctx", "fy", "core"),
    )
    acts = P(DP, PLANE, None)
    mats = P(ALL, None)
    vecs = P(None, ALL)
    ladder = sizes["dp"] == 4 and sizes["ctx"] == 2 and sizes["fsdp"] == 4
    return jax.shard_map(
        ladder_shards if ladder else wide_shards,
        mesh=fine,
        in_specs=(acts, P(DP, PLANE), acts) + (mats,) * 4 + (vecs,) + (mats,) * 8 + (vecs,) * 2,
        out_specs=(acts, acts) + (mats,) * 12 + (vecs,) * 3,
        check_vma=False,
    )
```

profile of v0, /device:TPU:0, one launch (start us, length us, event | category | flops | bytes accessed | tf_op | source)
XLA Modules:
  0.0 762.0 jit_solution(567773392033578614)
XLA Ops:
  12.6 16.0 %all_to_all.45 = bf16[8,80,512]{2,1,0:T(8,128)(2,1)} all-to-all(bf16[8,80,512]{2,1,0:T(8,128)(2,1)S(1)} %copy.162), channel_id=1, replica_groups=mesh['dh'=2,'dl'=2,'ctx'=2,'fy'=2,'core'=2] {'ctx','fy','core'}, dimensions={0} | all-to-all | bytes 1310720 | tf_op jit(solution)/shard_map/all_to_all | solution.py:98
  33.3 4.7 collective-permute-done.8
  44.3 7.3 collective-permute-done.12
  53.1 7.1 collective-permute-done.13
  66.0 6.7 copy.164
  80.2 9.8 %collective-permute-done.5 = bf16[128,2304]{1,0:T(8,128)(2,1)S(1)} collective-permute-done((bf16[128,2304]{1,0:T(8,128)(2,1)}, bf16[128,2304]{1,0:T(8,128)(2,1)S(1)}, u32[]{:S(2)}, u32[]{:S(2)}) %collective-permute-start.5) | collective-permute-done | bytes 589856 | tf_op jit(solution)/shard_map/ppermute | solution.py:106
  95.2 11.2 %all-gather.7.cloned.1.call-done = bf16[32,80,512]{2,1,0:T(8,128)(2,1)} async-done(((bf16[8,80,512]{2,1,0:T(8,128)(2,1)}), bf16[32,80,512]{2,1,0:T(8,128)(2,1)}) %all-gather.7.cloned.1.call-update) | async-done | bytes 2621456 | tf_op jit(solution)/shard_map/all_gather | solution.py:294
  138.9 4.5 all-to-all-done.1
  154.6 28.2 %all-to-all-done.2 = bf16[8,128,256]{1,2,0:T(8,128)(2,1)S(1)} async-done(((bf16[8,128,256]{1,2,0:T(8,128)(2,1)}), bf16[8,128,256]{1,2,0:T(8,128)(2,1)S(1)}, u32[]{:S(2)}, u32[]{:S(2)}) %all-to-all-start.2) | async-done | bytes 524320 | tf_op jit(solution)/shard_map/all_to_all | solution.py:98
  190.2 5.8 all-to-all-start.3
  196.9 4.6 broadcast_in_dim.130
  205.3 5.2 multiply_reduce_fusion.6
  214.4 14.9 %all-to-all-done.3 = bf16[8,72,1152]{2,1,0:T(8,128)(2,1)} async-done(((bf16[8,72,1152]{2,1,0:T(8,128)(2,1)}), bf16[8,72,1152]{2,1,0:T(8,128)(2,1)}, u32[]{:S(2)}, u32[]{:S(2)}) %all-to-all-start.3) | async-done | bytes 1327136 | tf_op jit(solution)/shard_map/all_to_all | solution.py:98
  237.0 4.6 collective-permute-start.16
  241.8 12.5 %collective-permute-done.17 = bf16[128,2304]{1,0:T(8,128)(2,1)S(1)} collective-permute-done((bf16[128,2304]{1,0:T(8,128)(2,1)S(1)}, bf16[128,2304]{1,0:T(8,128)(2,1)S(1)}, u32[]{:S(2)}, u32[]{:S(2)}) %collective-permute-start.17) | collective-permute-done | bytes 589856 | tf_op jit(solution)/shard_map/ppermute | solution.py:164
  272.2 7.1 collective-permute-done.20
  282.0 13.5 %fusion.145 = f32[1024,2304]{1,0:T(8,128)S(1)} fusion(bf16[1024,2304]{1,0:T(8,128)(2,1)S(1)} %constant_dynamic-update-slice_fusion, bf16[2304,2304]{1,0:T(8,128)(2,1)} %bitcast.50), kind=kOutput, calls=%fused_computation.354 | convolution fusion | flops 10871635968 | bytes 24772608 | tf_op jit(solution)/shard_map/dot_general | solution.py:38
  299.2 9.9 %convolution_convert_fusion.4 = bf16[1024,2304]{1,0:T(8,128)(2,1)S(1)} fusion(bf16[1024,1152]{1,0:T(8,128)(2,1)S(1)} %fusion.16, bf16[1152,2304]{1,0:T(8,128)(2,1)} %bitcast.56), kind=kOutput, calls=%fused_computation.17 | convolution fusion | flops 5438177280 | bytes 12386304 | tf_op jit(solution)/shard_map/dot_general | solution.py:38
  311.3 5.0 collective-permute-done.32
  320.8 11.0 %collective-permute-done.33 = bf16[128,2304]{1,0:T(8,128)(2,1)S(1)} collective-permute-done((bf16[128,2304]{1,0:T(8,128)(2,1)S(1)}, bf16[128,2304]{1,0:T(8,128)(2,1)S(1)}, u32[]{:S(2)}, u32[]{:S(2)}) %collective-permute-start.33) | collective-permute-done | bytes 589856 | tf_op jit(solution)/shard_map/ppermute | solution.py:207
  334.3 9.9 %collective-permute-done.35 = bf16[128,2304]{1,0:T(8,128)(2,1)S(1)} collective-permute-done((bf16[128,2304]{1,0:T(8,128)(2,1)S(1)}, bf16[128,2304]{1,0:T(8,128)(2,1)S(1)}, u32[]{:S(2)}, u32[]{:S(2)}) %collective-permute-start.35) | collective-permute-done | bytes 589856 | tf_op jit(solution)/shard_map/ppermute | solution.py:207
  351.3 11.1 %all-to-all-done.4 = bf16[8,128,256]{1,2,0:T(8,128)(2,1)S(1)} async-done(((bf16[8,128,256]{1,2,0:T(8,128)(2,1)}), bf16[8,128,256]{1,2,0:T(8,128)(2,1)S(1)}, u32[]{:S(2)}, u32[]{:S(2)}) %all-to-all-start.4) | async-done | bytes 524320 | tf_op jit(solution)/shard_map/all_to_all | solution.py:98
  369.2 12.3 %collective-permute-done.40 = bf16[128,2304]{1,0:T(8,128)(2,1)S(1)} collective-permute-done((bf16[128,2304]{1,0:T(8,128)(2,1)S(1)}, bf16[128,2304]{1,0:T(8,128)(2,1)S(1)}, u32[]{:S(2)}, u32[]{:S(2)}) %collective-permute-start.40) | collective-permute-done | bytes 589856 | tf_op jit(solution)/shard_map/ppermute | solution.py:164
  383.7 11.4 %collective-permute-done.42 = bf16[128,2304]{1,0:T(8,128)(2,1)S(1)} collective-permute-done((bf16[128,2304]{1,0:T(8,128)(2,1)S(1)}, bf16[128,2304]{1,0:T(8,128)(2,1)S(1)}, u32[]{:S(2)}, u32[]{:S(2)}) %collective-permute-start.42) | collective-permute-done | bytes 589856 | tf_op jit(solution)/shard_map/ppermute | solution.py:164
  397.5 9.8 %fusion.30 = (bf16[640,1152]{1,0:T(8,128)(2,1)S(1)}, bf16[640,1152]{1,0:T(8,128)(2,1)S(1)}) fusion(f32[1024,2304]{1,0:T(8,128)} %copy-done.8, bf16[640,2304]{1,0:T(8,128)(2,1)S(1)} %constant_dynamic-update-slice_fusion.9, bf16[1152,2304]{1,0:T(8,128)(2,1)} %bitcast.56), kind=kOutput, calls=%fused_computation.63 | convolution fusion | flops 3415080960 | bytes 17104896 | tf_op jit(solution)/shard_map/dot_general | solution.py:38
  410.5 10.5 %convolution_convert_fusion.5 = bf16[640,2304]{1,0:T(8,128)(2,1)S(1)} fusion(bf16[640,2304]{1,0:T(8,128)(2,1)S(1)} %pad_maximum_fusion, bf16[2304,2304]{1,0:T(8,128)(2,1)} %bitcast.50), kind=kOutput, calls=%fused_computation.26 | convolution fusion | flops 6796247040 | bytes 16515072 | tf_op jit(solution)/shard_map/dot_general | solution.py:38
  421.2 7.4 fusion.43
  428.7 8.3 %convolution_convert_fusion.7 = bf16[384,2304]{1,0:T(8,128)(2,1)S(1)} fusion(bf16[384,2304]{1,0:T(8,128)(2,1)S(1)} %pad_maximum_fusion.2, bf16[2304,2304]{1,0:T(8,128)(2,1)} %bitcast.50), kind=kOutput, calls=%fused_computation.44 | convolution fusion | flops 4077748224 | bytes 14155776 | tf_op jit(solution)/shard_map/dot_general | solution.py:38
  439.6 4.4 collective-permute-done.48
  451.3 8.0 %convolution_convert_fusion.1 = bf16[2304,1152]{1,0:T(8,128)(2,1)} fusion(bf16[1024,2304]{1,0:T(8,128)(2,1)S(1)} %bitcast.333, bf16[1024,2304]{1,0:T(8,128)(2,1)S(1)} %constant_dynamic-update-slice_fusion.18), kind=kOutput, calls=%fused_computation.1 | convolution fusion | flops 5438472192 | bytes 12386304 | tf_op jit(solution)/shard_map/dot_general | solution.py:38
  466.2 8.0 %convolution_convert_fusion.2 = bf16[2304,1152]{1,0:T(8,128)(2,1)} fusion(bf16[1024,2304]{1,0:T(8,128)(2,1)S(1)} %bitcast.333, bf16[1024,2304]{1,0:T(8,128)(2,1)S(1)} %constant_dynamic-update-slice_fusion.18), kind=kOutput, calls=%fused_computation.2 | convolution fusion | flops 5438472192 | bytes 12386304 | tf_op jit(solution)/shard_map/dot_general | solution.py:38
  474.3 5.2 collective-permute-done.51
  483.0 7.5 convolution_convert_fusion
  495.2 6.8 convolution_convert_fusion.9
  507.3 4.5 dynamic-slice_bitcast_fusion.4
  511.8 6.6 all-to-all-done.5
  519.9 4.7 multiply_convert_fusion
  545.2 4.9 slice.360
  551.3 4.9 convolution_convert_fusion.8
  556.1 6.2 convolution_convert_fusion.6
  569.1 4.6 convolution_convert_fusion.3
  588.8 25.1 %collective-permute-done.60 = bf16[8,72,1152]{2,1,0:T(8,128)(2,1)} collective-permute-done((bf16[8,72,1152]{2,1,0:T(8,128)(2,1)}, bf16[8,72,1152]{2,1,0:T(8,128)(2,1)}, u32[]{:S(2)}, u32[]{:S(2)}) %collective-permute-start.60) | collective-permute-done | bytes 1327136 | tf_op jit(solution)/shard_map/ppermute | solution.py:106
  616.7 5.4 all-to-all-start.6
  631.3 16.6 %collective-permute-done.62 = bf16[64,2304]{1,0:T(8,128)(2,1)S(1)} collective-permute-done((bf16[64,2304]{1,0:T(8,128)(2,1)S(1)}, bf16[64,2304]{1,0:T(8,128)(2,1)S(1)}, u32[]{:S(2)}, u32[]{:S(2)}) %collective-permute-start.62) | collective-permute-done | bytes 294944 | tf_op jit(solution)/shard_map/ppermute | solution.py:106
  650.9 27.0 %all-to-all-done.6 = bf16[8,72,1152]{2,1,0:T(8,128)(2,1)} async-done(((bf16[8,72,1152]{2,1,0:T(8,128)(2,1)}), bf16[8,72,1152]{2,1,0:T(8,128)(2,1)}, u32[]{:S(2)}, u32[]{:S(2)}) %all-to-all-start.6) | async-done | bytes 1327136 | tf_op jit(solution)/shard_map/all_to_all | solution.py:98
  692.7 20.6 %collective-permute-done.66 = bf16[1,288,2304]{2,1,0:T(8,128)(2,1)S(1)} collective-permute-done((bf16[1,288,2304]{2,1,0:T(8,128)(2,1)}, bf16[1,288,2304]{2,1,0:T(8,128)(2,1)S(1)}, u32[]{:S(2)}, u32[]{:S(2)}) %collective-permute-start.66) | collective-permute-done | bytes 1327136 | tf_op jit(solution)/shard_map/ppermute | solution.py:106
  713.4 7.0 convert_subtract_fusion.1
  735.4 12.5 %convert_subtract_fusion = (f32[72,18432]{1,0:T(8,128)}, f32[72,18432]{1,0:T(8,128)}, f32[72,18432]{1,0:T(8,128)}, f32[72]{0:T(128)S(1)}) fusion(bf16[72,18432]{1,0:T(8,128)(2,1)S(1)} %copy-done.6, bf16[72,9216]{1,0:T(8,128)(2,1)} %bitcast.299, bf16[72,9216]{1,0:T(8,128)(2,1)S(1)} %bitcast.298, f32[72,18432]{1,0:T(8,128)} %param.30, f32[72,18432]{1,0:T(8,128)} %param.31), kind=kLoop, calls=%fused_computation.11 | loop fusion | flops 29196216 | bytes 31850784 | tf_op jit(solution)/shard_map/sub | solution.py:86
  (483 shorter events, 282.4 us)
Async XLA Ops:
  7.2 99.1 %all-gather.7.cloned.1.call-start = ((), (), s32[]{:S(2)}) async-start(), calls=%async_computation.11 | async-start | bytes 3276800 | tf_op jit(solution)/shard_map/all_gather | solution.py:294
  44.2 161.1 %all-gather.9.cloned.1.call-start = ((), (), s32[]{:S(2)}) async-start(), calls=%async_computation.12 | async-start | bytes 10616832 | tf_op jit(solution)/shard_map/all_gather | solution.py:304
  63.7 13.7 %collective-permute-start.3 = (bf16[128,2304]{1,0:T(8,128)(2,1)S(1)}, bf16[128,2304]{1,0:T(8,128)(2,1)S(1)}, u32[]{:S(2)}, u32[]{:S(2)}) collective-permute-start(bf16[128,2304]{1,0:T(8,128)(2,1)S(1)} %bitcast.292), channel_id=1, source_target_pairs={{0,4},{4,0},{1,5},{5,1},{2,6},{6,2},{3,7},{7,3},{8,12},{12,8},{9,1... | collective-permute-start | bytes 1769480 | tf_op jit(solution)/shard_map/ppermute | solution.py:106
  107.5 35.9 %all-to-all-start.1 = ((bf16[8,72,1152]{2,1,0:T(8,128)(2,1)}), bf16[8,72,1152]{2,1,0:T(8,128)(2,1)S(1)}, u32[]{:S(2)}, u32[]{:S(2)}) async-start(bf16[8,72,1152]{2,1,0:T(8,128)(2,1)} %copy.163), calls=%async_computation.1 | async-start | bytes 2654208 | tf_op jit(solution)/shard_map/all_to_all | solution.py:98
  129.5 99.8 %collective-permute-start.29 = (bf16[1,288,2304]{2,1,0:T(8,128)(2,1)}, bf16[1,288,2304]{2,1,0:T(8,128)(2,1)}, u32[]{:S(2)}, u32[]{:S(2)}) collective-permute-start(bf16[1,288,2304]{2,1,0:T(8,128)(2,1)} %bitcast.52), channel_id=1, source_target_pairs={{0,2},{2,0},{1,3},{3,1},{4,6},{6,4},{5,7},{7,5},{8,10},{10,8},{9,1... | collective-permute-start | bytes 3981320 | tf_op jit(solution)/shard_map/ppermute | solution.py:106
  131.1 51.7 %collective-permute-start.28 = (bf16[1,288,2304]{2,1,0:T(8,128)(2,1)}, bf16[1,288,2304]{2,1,0:T(8,128)(2,1)}, u32[]{:S(2)}, u32[]{:S(2)}) collective-permute-start(bf16[1,288,2304]{2,1,0:T(8,128)(2,1)} %bitcast.52), channel_id=1, source_target_pairs={{0,1},{1,0},{2,3},{3,2},{4,5},{5,4},{6,7},{7,6},{8,9},{9,8},{10,11... | collective-permute-start | bytes 3981320 | tf_op jit(solution)/shard_map/ppermute | solution.py:106
  145.8 37.1 %all-to-all-start.2 = ((bf16[8,128,256]{1,2,0:T(8,128)(2,1)}), bf16[8,128,256]{1,2,0:T(8,128)(2,1)S(1)}, u32[]{:S(2)}, u32[]{:S(2)}) async-start(bf16[8,128,256]{1,2,0:T(8,128)(2,1)} %copy_bitcast_fusion.1), calls=%async_computation.2 | async-start | bytes 1048576 | tf_op jit(solution)/shard_map/all_to_all | solution.py:98
  182.9 19.8 %collective-permute-start.22 = (bf16[8,72,1152]{2,1,0:T(8,128)(2,1)}, bf16[8,72,1152]{2,1,0:T(8,128)(2,1)}, u32[]{:S(2)}, u32[]{:S(2)}) collective-permute-start(bf16[8,72,1152]{2,1,0:T(8,128)(2,1)} %copy-done.14), channel_id=1, source_target_pairs={{0,1},{1,0},{2,3},{3,2},{4,5},{5,4},{6,7},{7,6},{8,9},{9,8},{10,11... | collective-permute-start | bytes 3981320 | tf_op jit(solution)/shard_map/ppermute | solution.py:106
  185.4 43.9 %collective-permute-start.23 = (bf16[8,72,1152]{2,1,0:T(8,128)(2,1)}, bf16[8,72,1152]{2,1,0:T(8,128)(2,1)}, u32[]{:S(2)}, u32[]{:S(2)}) collective-permute-start(bf16[8,72,1152]{2,1,0:T(8,128)(2,1)} %copy-done.14), channel_id=1, source_target_pairs={{0,2},{2,0},{1,3},{3,1},{4,6},{6,4},{5,7},{7,5},{8,10},{10,8},{9,1... | collective-permute-start | bytes 3981320 | tf_op jit(solution)/shard_map/ppermute | solution.py:106
  190.2 39.1 %all-to-all-start.3 = ((bf16[8,72,1152]{2,1,0:T(8,128)(2,1)}), bf16[8,72,1152]{2,1,0:T(8,128)(2,1)}, u32[]{:S(2)}, u32[]{:S(2)}) async-start(bf16[8,72,1152]{2,1,0:T(8,128)(2,1)} %copy.168), calls=%async_computation.3 | async-start | bytes 2654208 | tf_op jit(solution)/shard_map/all_to_all | solution.py:98
  212.3 23.1 %collective-permute-start.15 = (bf16[128,2304]{1,0:T(8,128)(2,1)}, bf16[128,2304]{1,0:T(8,128)(2,1)S(1)}, u32[]{:S(2)}, u32[]{:S(2)}) collective-permute-start(bf16[128,2304]{1,0:T(8,128)(2,1)} %get-tuple-element.172), channel_id=1, source_target_pairs={{8,0},{16,8},{24,16},{28,24},{20,28},{12,20},{4,12},{0,4},{9,1},{1... | collective-permute-start | bytes 1769480 | tf_op jit(solution)/shard_map/ppermute | solution.py:164
  214.4 22.7 %collective-permute-start.14 = (bf16[128,2304]{1,0:T(8,128)(2,1)}, bf16[128,2304]{1,0:T(8,128)(2,1)S(1)}, u32[]{:S(2)}, u32[]{:S(2)}) collective-permute-start(bf16[128,2304]{1,0:T(8,128)(2,1)} %get-tuple-element.172), channel_id=1, source_target_pairs={{0,8},{8,16},{16,24},{24,28},{28,20},{20,12},{12,4},{4,0},{1,9},{9... | collective-permute-start | bytes 1769480 | tf_op jit(solution)/shard_map/ppermute | solution.py:163
  229.3 35.7 %collective-permute-start.30 = (bf16[1,288,2304]{2,1,0:T(8,128)(2,1)}, bf16[1,288,2304]{2,1,0:T(8,128)(2,1)S(1)}, u32[]{:S(2)}, u32[]{:S(2)}) collective-permute-start(bf16[1,288,2304]{2,1,0:T(8,128)(2,1)} %collective-permute-done.29), channel_id=1, source_target_pairs={{0,1},{1,0},{2,3},{3,2},{4,5},{5,4},{6,7},{7,6},{8,9},{9,8},{10,11... | collective-permute-start | bytes 3981320 | tf_op jit(solution)/shard_map/ppermute | solution.py:106
  229.4 27.5 %collective-permute-start.24 = (bf16[8,72,1152]{2,1,0:T(8,128)(2,1)}, bf16[8,72,1152]{2,1,0:T(8,128)(2,1)S(1)}, u32[]{:S(2)}, u32[]{:S(2)}) collective-permute-start(bf16[8,72,1152]{2,1,0:T(8,128)(2,1)} %collective-permute-done.23), channel_id=1, source_target_pairs={{0,1},{1,0},{2,3},{3,2},{4,5},{5,4},{6,7},{7,6},{8,9},{9,8},{10,11... | collective-permute-start | bytes 3981320 | tf_op jit(solution)/shard_map/ppermute | solution.py:106
  229.9 31.3 %collective-permute-start.26 = (bf16[8,72,1152]{2,1,0:T(8,128)(2,1)}, bf16[8,72,1152]{2,1,0:T(8,128)(2,1)S(1)}, u32[]{:S(2)}, u32[]{:S(2)}) collective-permute-start(bf16[8,72,1152]{2,1,0:T(8,128)(2,1)} %all-to-all-done.3), channel_id=1, source_target_pairs={{0,2},{2,0},{1,3},{3,1},{4,6},{6,4},{5,7},{7,5},{8,10},{10,8},{9,1... | collective-permute-start | bytes 3981320 | tf_op jit(solution)/shard_map/ppermute | solution.py:106
  235.5 18.8 %collective-permute-start.17 = (bf16[128,2304]{1,0:T(8,128)(2,1)S(1)}, bf16[128,2304]{1,0:T(8,128)(2,1)S(1)}, u32[]{:S(2)}, u32[]{:S(2)}) collective-permute-start(bf16[128,2304]{1,0:T(8,128)(2,1)S(1)} %collective-permute-done.15), channel_id=1, source_target_pairs={{8,0},{16,8},{24,16},{28,24},{20,28},{12,20},{4,12},{0,4},{9,1},{1... | collective-permute-start | bytes 1769480 | tf_op jit(solution)/shard_map/ppermute | solution.py:164
  237.0 17.4 %collective-permute-start.16 = (bf16[128,2304]{1,0:T(8,128)(2,1)S(1)}, bf16[128,2304]{1,0:T(8,128)(2,1)S(1)}, u32[]{:S(2)}, u32[]{:S(2)}) collective-permute-start(bf16[128,2304]{1,0:T(8,128)(2,1)S(1)} %collective-permute-done.14), channel_id=1, source_target_pairs={{0,8},{8,16},{16,24},{24,28},{28,20},{20,12},{12,4},{4,0},{1,9},{9... | collective-permute-start | bytes 1769480 | tf_op jit(solution)/shard_map/ppermute | solution.py:163
  254.5 15.5 %collective-permute-start.19 = (bf16[128,2304]{1,0:T(8,128)(2,1)S(1)}, bf16[128,2304]{1,0:T(8,128)(2,1)S(1)}, u32[]{:S(2)}, u32[]{:S(2)}) collective-permute-start(bf16[128,2304]{1,0:T(8,128)(2,1)S(1)} %collective-permute-done.17), channel_id=1, source_target_pairs={{8,0},{16,8},{24,16},{28,24},{20,28},{12,20},{4,12},{0,4},{9,1},{1... | collective-permute-start | bytes 1769480 | tf_op jit(solution)/shard_map/ppermute | solution.py:164
  256.9 14.4 %collective-permute-start.18 = (bf16[128,2304]{1,0:T(8,128)(2,1)S(1)}, bf16[128,2304]{1,0:T(8,128)(2,1)S(1)}, u32[]{:S(2)}, u32[]{:S(2)}) collective-permute-start(bf16[128,2304]{1,0:T(8,128)(2,1)S(1)} %collective-permute-done.16), channel_id=1, source_target_pairs={{0,8},{8,16},{16,24},{24,28},{28,20},{20,12},{12,4},{4,0},{1,9},{9... | collective-permute-start | bytes 1769480 | tf_op jit(solution)/shard_map/ppermute | solution.py:163
  261.2 18.2 %collective-permute-start.27 = (bf16[8,72,1152]{2,1,0:T(8,128)(2,1)S(1)}, bf16[8,72,1152]{2,1,0:T(8,128)(2,1)S(1)}, u32[]{:S(2)}, u32[]{:S(2)}) collective-permute-start(bf16[8,72,1152]{2,1,0:T(8,128)(2,1)S(1)} %collective-permute-done.26), channel_id=1, source_target_pairs={{0,1},{1,0},{2,3},{3,2},{4,5},{5,4},{6,7},{7,6},{8,9},{9,8},{10,11... | collective-permute-start | bytes 3981320 | tf_op jit(solution)/shard_map/ppermute | solution.py:106
  345.6 17.8 %collective-permute-start.37 = (bf16[128,2304]{1,0:T(8,128)(2,1)}, bf16[128,2304]{1,0:T(8,128)(2,1)}, u32[]{:S(2)}, u32[]{:S(2)}) collective-permute-start(bf16[128,2304]{1,0:T(8,128)(2,1)} %get-tuple-element.98), channel_id=1, source_target_pairs={{0,8},{8,16},{16,24},{24,28},{28,20},{20,12},{12,4},{4,0},{1,9},{9... | collective-permute-start | bytes 1769480 | tf_op jit(solution)/shard_map/ppermute | solution.py:207
  346.3 17.1 %collective-permute-start.38 = (bf16[128,2304]{1,0:T(8,128)(2,1)}, bf16[128,2304]{1,0:T(8,128)(2,1)}, u32[]{:S(2)}, u32[]{:S(2)}) collective-permute-start(bf16[128,2304]{1,0:T(8,128)(2,1)} %get-tuple-element.99), channel_id=1, source_target_pairs={{8,0},{16,8},{24,16},{28,24},{20,28},{12,20},{4,12},{0,4},{9,1},{1... | collective-permute-start | bytes 1769480 | tf_op jit(solution)/shard_map/ppermute | solution.py:208
  347.6 14.7 %all-to-all-start.4 = ((bf16[8,128,256]{1,2,0:T(8,128)(2,1)}), bf16[8,128,256]{1,2,0:T(8,128)(2,1)S(1)}, u32[]{:S(2)}, u32[]{:S(2)}) async-start(bf16[8,128,256]{1,2,0:T(8,128)(2,1)} %bitcast.38), calls=%async_computation.4 | async-start | bytes 1048576 | tf_op jit(solution)/shard_map/all_to_all | solution.py:98
  351.1 194.1 %all-gather.11.cloned.1.call-start = ((), (), s32[]{:S(2)}) async-start(), calls=%async_computation.13 | async-start | bytes 5971968 | tf_op jit(solution)/shard_map/all_gather | solution.py:395
  367.1 14.4 %collective-permute-start.40 = (bf16[128,2304]{1,0:T(8,128)(2,1)S(1)}, bf16[128,2304]{1,0:T(8,128)(2,1)S(1)}, u32[]{:S(2)}, u32[]{:S(2)}) collective-permute-start(bf16[128,2304]{1,0:T(8,128)(2,1)S(1)} %get-tuple-element.170), channel_id=1, source_target_pairs={{8,0},{16,8},{24,16},{28,24},{20,28},{12,20},{4,12},{0,4},{9,1},{1... | collective-permute-start | bytes 1769480 | tf_op jit(solution)/shard_map/ppermute | solution.py:164
  368.9 14.4 %collective-permute-start.39 = (bf16[128,2304]{1,0:T(8,128)(2,1)S(1)}, bf16[128,2304]{1,0:T(8,128)(2,1)S(1)}, u32[]{:S(2)}, u32[]{:S(2)}) collective-permute-start(bf16[128,2304]{1,0:T(8,128)(2,1)S(1)} %get-tuple-element.170), channel_id=1, source_target_pairs={{0,8},{8,16},{16,24},{24,28},{28,20},{20,12},{12,4},{4,0},{1,9},{9... | collective-permute-start | bytes 1769480 | tf_op jit(solution)/shard_map/ppermute | solution.py:163
  381.5 13.5 %collective-permute-start.42 = (bf16[128,2304]{1,0:T(8,128)(2,1)S(1)}, bf16[128,2304]{1,0:T(8,128)(2,1)S(1)}, u32[]{:S(2)}, u32[]{:S(2)}) collective-permute-start(bf16[128,2304]{1,0:T(8,128)(2,1)S(1)} %collective-permute-done.40), channel_id=1, source_target_pairs={{8,0},{16,8},{24,16},{28,24},{20,28},{12,20},{4,12},{0,4},{9,1},{1... | collective-permute-start | bytes 1769480 | tf_op jit(solution)/shard_map/ppermute | solution.py:164
  383.3 13.5 %collective-permute-start.41 = (bf16[128,2304]{1,0:T(8,128)(2,1)S(1)}, bf16[128,2304]{1,0:T(8,128)(2,1)S(1)}, u32[]{:S(2)}, u32[]{:S(2)}) collective-permute-start(bf16[128,2304]{1,0:T(8,128)(2,1)S(1)} %collective-permute-done.39), channel_id=1, source_target_pairs={{0,8},{8,16},{16,24},{24,28},{28,20},{20,12},{12,4},{4,0},{1,9},{9... | collective-permute-start | bytes 1769480 | tf_op jit(solution)/shard_map/ppermute | solution.py:163
  449.1 14.1 %collective-permute-start.49 = (bf16[128,2304]{1,0:T(8,128)(2,1)S(1)}, bf16[128,2304]{1,0:T(8,128)(2,1)S(1)}, u32[]{:S(2)}, u32[]{:S(2)}) collective-permute-start(bf16[128,2304]{1,0:T(8,128)(2,1)S(1)} %pad_maximum_fusion.8), channel_id=1, source_target_pairs={{0,8},{8,16},{16,24},{24,28},{28,20},{20,12},{12,4},{4,0},{1,9},{9... | collective-permute-start | bytes 1769480 | tf_op jit(solution)/shard_map/ppermute | solution.py:207
  449.2 14.4 %collective-permute-start.50 = (bf16[128,2304]{1,0:T(8,128)(2,1)S(1)}, bf16[128,2304]{1,0:T(8,128)(2,1)S(1)}, u32[]{:S(2)}, u32[]{:S(2)}) collective-permute-start(bf16[128,2304]{1,0:T(8,128)(2,1)S(1)} %pad_maximum_fusion.9), channel_id=1, source_target_pairs={{8,0},{16,8},{24,16},{28,24},{20,28},{12,20},{4,12},{0,4},{9,1},{1... | collective-permute-start | bytes 1769480 | tf_op jit(solution)/shard_map/ppermute | solution.py:208
  463.9 15.6 %collective-permute-start.51 = (bf16[128,2304]{1,0:T(8,128)(2,1)S(1)}, bf16[128,2304]{1,0:T(8,128)(2,1)S(1)}, u32[]{:S(2)}, u32[]{:S(2)}) collective-permute-start(bf16[128,2304]{1,0:T(8,128)(2,1)S(1)} %get-tuple-element.108), channel_id=1, source_target_pairs={{0,8},{8,16},{16,24},{24,28},{28,20},{20,12},{12,4},{4,0},{1,9},{9... | collective-permute-start | bytes 1769480 | tf_op jit(solution)/shard_map/ppermute | solution.py:207
  465.0 15.6 %collective-permute-start.52 = (bf16[128,2304]{1,0:T(8,128)(2,1)S(1)}, bf16[128,2304]{1,0:T(8,128)(2,1)S(1)}, u32[]{:S(2)}, u32[]{:S(2)}) collective-permute-start(bf16[128,2304]{1,0:T(8,128)(2,1)S(1)} %get-tuple-element.109), channel_id=1, source_target_pairs={{8,0},{16,8},{24,16},{28,24},{20,28},{12,20},{4,12},{0,4},{9,1},{1... | collective-permute-start | bytes 1769480 | tf_op jit(solution)/shard_map/ppermute | solution.py:208
  503.1 15.3 %all-to-all-start.5 = ((bf16[8,128,256]{1,2,0:T(8,128)(2,1)}), bf16[8,128,256]{1,2,0:T(8,128)(2,1)}, u32[]{:S(2)}, u32[]{:S(2)}) async-start(bf16[8,128,256]{1,2,0:T(8,128)(2,1)} %bitcast.62), calls=%async_computation.5 | async-start | bytes 1048576 | tf_op jit(solution)/shard_map/all_to_all | solution.py:98
  507.2 213.2 %reduce-scatter.2.cloned.1.call-start = ((), (), s32[]{:S(2)}) async-start(), calls=%async_computation.10 | async-start | bytes 4464640 | tf_op jit(solution)/shard_map/reduce_scatter | solution.py:94
  530.9 52.0 %collective-permute-start.57 = (bf16[8,2,72,1152]{3,2,1,0:T(8,128)(2,1)}, bf16[8,2,72,1152]{3,2,1,0:T(8,128)(2,1)}, u32[]{:S(2)}, u32[]{:S(2)}) collective-permute-start(bf16[8,2,72,1152]{3,2,1,0:T(8,128)(2,1)} %get-tuple-element.182), channel_id=1, source_target_pairs={{0,1},{1,0},{2,3},{3,2},{4,5},{5,4},{6,7},{7,6},{8,9},{9,8},{10,11... | collective-permute-start | bytes 7962632 | tf_op jit(solution)/shard_map/ppermute | solution.py:106
  531.4 57.5 %collective-permute-start.56 = (bf16[1,2,288,2304]{3,2,1,0:T(8,128)(2,1)}, bf16[1,2,288,2304]{3,2,1,0:T(8,128)(2,1)}, u32[]{:S(2)}, u32[]{:S(2)}) collective-permute-start(bf16[1,2,288,2304]{3,2,1,0:T(8,128)(2,1)} %get-tuple-element.184), channel_id=1, source_target_pairs={{0,1},{1,0},{2,3},{3,2},{4,5},{5,4},{6,7},{7,6},{8,9},{9,8},{10,11... | collective-permute-start | bytes 7962632 | tf_op jit(solution)/shard_map/ppermute | solution.py:106
  535.0 40.7 %collective-permute-start.59 = (bf16[8,2,72,1152]{3,2,1,0:T(8,128)(2,1)}, bf16[8,2,72,1152]{3,2,1,0:T(8,128)(2,1)}, u32[]{:S(2)}, u32[]{:S(2)}) collective-permute-start(bf16[8,2,72,1152]{3,2,1,0:T(8,128)(2,1)} %get-tuple-element.180), channel_id=1, source_target_pairs={{0,1},{1,0},{2,3},{3,2},{4,5},{5,4},{6,7},{7,6},{8,9},{9,8},{10,11... | collective-permute-start | bytes 7962632 | tf_op jit(solution)/shard_map/ppermute | solution.py:106
  575.4 46.8 %collective-permute-start.61 = (bf16[4,128,2304]{2,1,0:T(8,128)(2,1)}, bf16[4,128,2304]{2,1,0:T(8,128)(2,1)}, u32[]{:S(2)}, u32[]{:S(2)}) collective-permute-start(bf16[4,128,2304]{2,1,0:T(8,128)(2,1)} %dynamic-slice_bitcast_fusion.6), channel_id=1, source_target_pairs={{0,1},{1,0},{2,3},{3,2},{4,5},{5,4},{6,7},{7,6},{8,9},{9,8},{10,11... | collective-permute-start | bytes 7077896 | tf_op jit(solution)/shard_map/ppermute | solution.py:106
  581.7 32.3 %collective-permute-start.60 = (bf16[8,72,1152]{2,1,0:T(8,128)(2,1)}, bf16[8,72,1152]{2,1,0:T(8,128)(2,1)}, u32[]{:S(2)}, u32[]{:S(2)}) collective-permute-start(bf16[8,72,1152]{2,1,0:T(8,128)(2,1)} %get-tuple-element.204), channel_id=1, source_target_pairs={{0,2},{2,0},{1,3},{3,1},{4,6},{6,4},{5,7},{7,5},{8,10},{10,8},{9,1... | collective-permute-start | bytes 3981320 | tf_op jit(solution)/shard_map/ppermute | solution.py:106
  587.8 63.0 %collective-permute-start.58 = (bf16[8,72,1152]{2,1,0:T(8,128)(2,1)}, bf16[8,72,1152]{2,1,0:T(8,128)(2,1)}, u32[]{:S(2)}, u32[]{:S(2)}) collective-permute-start(bf16[8,72,1152]{2,1,0:T(8,128)(2,1)} %get-tuple-element.206), channel_id=1, source_target_pairs={{0,2},{2,0},{1,3},{3,1},{4,6},{6,4},{5,7},{7,5},{8,10},{10,8},{9,1... | collective-permute-start | bytes 3981320 | tf_op jit(solution)/shard_map/ppermute | solution.py:106
  616.7 61.1 %all-to-all-start.6 = ((bf16[8,72,1152]{2,1,0:T(8,128)(2,1)}), bf16[8,72,1152]{2,1,0:T(8,128)(2,1)}, u32[]{:S(2)}, u32[]{:S(2)}) async-start(bf16[8,72,1152]{2,1,0:T(8,128)(2,1)} %add_convert_fusion.5), calls=%async_computation.7 | async-start | bytes 2654208 | tf_op jit(solution)/shard_map/all_to_all | solution.py:98
  625.3 22.7 %collective-permute-start.62 = (bf16[64,2304]{1,0:T(8,128)(2,1)S(1)}, bf16[64,2304]{1,0:T(8,128)(2,1)S(1)}, u32[]{:S(2)}, u32[]{:S(2)}) collective-permute-start(bf16[64,2304]{1,0:T(8,128)(2,1)S(1)} %get-tuple-element.211), channel_id=1, source_target_pairs={{0,2},{2,0},{1,3},{3,1},{4,6},{6,4},{5,7},{7,5},{8,10},{10,8},{9,1... | collective-permute-start | bytes 884744 | tf_op jit(solution)/shard_map/ppermute | solution.py:106
  625.5 22.4 %collective-permute-start.64 = (bf16[64,2304]{1,0:T(8,128)(2,1)S(1)}, bf16[64,2304]{1,0:T(8,128)(2,1)S(1)}, u32[]{:S(2)}, u32[]{:S(2)}) collective-permute-start(bf16[64,2304]{1,0:T(8,128)(2,1)S(1)} %get-tuple-element.213), channel_id=1, source_target_pairs={{0,4},{4,0},{1,5},{5,1},{2,6},{6,2},{3,7},{7,3},{8,12},{12,8},{9,1... | collective-permute-start | bytes 884744 | tf_op jit(solution)/shard_map/ppermute | solution.py:106
  648.2 40.2 %collective-permute-start.65 = (bf16[128,2304]{1,0:T(8,128)(2,1)S(1)}, bf16[128,2304]{1,0:T(8,128)(2,1)}, u32[]{:S(2)}, u32[]{:S(2)}) collective-permute-start(bf16[128,2304]{1,0:T(8,128)(2,1)S(1)} %pad_maximum_fusion.11), channel_id=1, source_target_pairs={{0,2},{2,0},{1,3},{3,1},{4,6},{6,4},{5,7},{7,5},{8,10},{10,8},{9,1... | collective-permute-start | bytes 1769480 | tf_op jit(solution)/shard_map/ppermute | solution.py:106
  650.3 38.1 %collective-permute-start.63 = (bf16[128,2304]{1,0:T(8,128)(2,1)}, bf16[128,2304]{1,0:T(8,128)(2,1)}, u32[]{:S(2)}, u32[]{:S(2)}) collective-permute-start(bf16[128,2304]{1,0:T(8,128)(2,1)} %pad_maximum_fusion.10), channel_id=1, source_target_pairs={{0,4},{4,0},{1,5},{5,1},{2,6},{6,2},{3,7},{7,3},{8,12},{12,8},{9,1... | collective-permute-start | bytes 1769480 | tf_op jit(solution)/shard_map/ppermute | solution.py:106
  682.6 30.7 %collective-permute-start.66 = (bf16[1,288,2304]{2,1,0:T(8,128)(2,1)}, bf16[1,288,2304]{2,1,0:T(8,128)(2,1)S(1)}, u32[]{:S(2)}, u32[]{:S(2)}) collective-permute-start(bf16[1,288,2304]{2,1,0:T(8,128)(2,1)} %get-tuple-element.202), channel_id=1, source_target_pairs={{0,2},{2,0},{1,3},{3,1},{4,6},{6,4},{5,7},{7,5},{8,10},{10,8},{9,1... | collective-permute-start | bytes 3981320 | tf_op jit(solution)/shard_map/ppermute | solution.py:106
  684.1 41.6 %all-to-all-start.7 = ((bf16[8,72,1152]{2,1,0:T(8,128)(2,1)}), bf16[8,72,1152]{2,1,0:T(8,128)(2,1)}, u32[]{:S(2)}, u32[]{:S(2)}) async-start(bf16[8,72,1152]{2,1,0:T(8,128)(2,1)} %add_convert_fusion.4), calls=%async_computation.8 | async-start | bytes 2654208 | tf_op jit(solution)/shard_map/all_to_all | solution.py:98
  729.2 20.4 %all-to-all-start.8 = ((bf16[8,72,512]{2,1,0:T(8,128)(2,1)}), bf16[8,72,512]{2,1,0:T(8,128)(2,1)S(1)}, u32[]{:S(2)}, u32[]{:S(2)}) async-start(bf16[8,72,512]{2,1,0:T(8,128)(2,1)} %bitcast.319), calls=%async_computation.9 | async-start | bytes 1179648 | tf_op jit(solution)/shard_map/all_to_all | solution.py:98
  (111 other events, 1135.5 us)
Sparse Core Ops, SparseCore 0:
  44.3 61.9 all-gather.6
  108.8 87.9 all-gather.8
  495.4 49.8 all-gather.10
  583.0 87.9 reduce-scatter.1
where the time goes:
time: 769 us; the launch traced here: 762 us
  waiting for transfers between devices  304 us (40%)
  matrix products  128 us (17%)
  local copies, waits for them, and re-layouts  109 us (14%)
  starting transfers between devices  99.2 us (13%)
  other arithmetic  87 us (11%)
  between operations  18.5 us (2%)
  blocking collectives  16 us (2%)
    dot_general x21, matrix products, dot(): lax.dot_general(left, right, (dims, ((), ())), preferred_element_type=jnp...  128 us
    all_to_all x8, waiting for transfers between devices, swap(): return lax.all_to_all(v, axes, split_axis=0, concat_axis=0, tiled=True)  92.3 us
    ppermute x29, waiting for transfers between devices, flip(): return lax.ppermute(v, axis, [(0, 1), (1, 0)])  81.4 us
    ppermute x6, waiting for transfers between devices, ring_gather(): ahead = lax.ppermute(ahead, LADDER, back)  38.1 us
    all_to_all x8, starting transfers between devices, swap(): return lax.all_to_all(v, axes, split_axis=0, concat_axis=0, tiled=True)  34.9 us
    ppermute x6, waiting for transfers between devices, ring_scatter(): ahead = lax.ppermute(to_ahead, LADDER, onward)  30.3 us
    convert_element_type x16, other arithmetic, bf(): return v.astype(jnp.bfloat16)  27.7 us
    sub x5, other arithmetic, adam_step(): return (weight - rate * (ratio + decay * weight), first_new, second_new)  24.2 us
  transfers between devices with their start and end apart: 79, of which 41 were waited for; matrix products, arithmetic and copies ran while one was open for 33% of the time, Pallas kernels for 0%

commit v1 on v0

--- a/solution.py
+++ b/solution.py
@@ -297,7 +297,7 @@
     for part in range(2):
         piece = w_gate_up[:, part * group * ff_own : (part + 1) * group * ff_own]
         cols.append(jnp.swapaxes(piece.reshape(rows, group, ff_own), 0, 1))
-    got, cols[0], w_down_late = hold((got, cols[0], w_down))
+    got, cols[0] = hold((got, cols[0]))
     w_own = got[:, :, :rows].reshape(width, 2 * HEAD_DIM)
     gain_vals = got[:, :, rows, : 4 * rows].reshape(planes * HEADS, 4, rows)
     gain_vals = f32(jnp.swapaxes(gain_vals, 0, 1).reshape(4, width))
@@ -333,7 +333,8 @@
     tokens_own = bf(normed_two)
     steps = ring_gather(tokens_own)
     cols[1], _ = hold((cols[1], tokens_own))
-    down_own = quad_place([quad_blocks(w_down_late[None], tokens_own)], 1).reshape(ff_own, width)
+    w_down_late, _ = hold((w_down, steps[2][0]))
+    down_own = quad_place([quad_blocks(w_down_late[None])], 1).reshape(ff_own, width)
     gate_up_own = [quad_blocks(cols[0], tokens_own), quad_blocks(cols[1])]
     gate_up_own = quad_place(gate_up_own, 2).reshape(width, 2 * ff_own)
     tokens = jnp.concatenate(sum(steps, []), axis=0)
@@ -348,7 +349,8 @@
     attn_cols = attn_own.reshape(tok, planes, HEADS, w_out.shape[0])
     attn_cols = jnp.transpose(attn_cols, (2, 0, 1, 3)).reshape(HEADS, tok, HEAD_DIM)
     attn_cols, down = hold((attn_cols, down))
-    attn_cols = swap(attn_cols, PLANE).reshape(HEADS * tok, HEAD_DIM)
+    attn_cols = swap(attn_cols, PLANE)
+    attn_cols = jnp.pad(attn_cols, ((0, 0), (0, 16), (0, 0))).reshape(-1, HEAD_DIM)
     down = ring_scatter(steps_of((down[:late], down[late:]), tok))
     down, attn_cols = hold((down, attn_cols))
     branch_two, pull_three = jax.vjp(rms_scale, down, gain_vals[3])
@@ -394,14 +396,17 @@
     others = jnp.concatenate([grad_mixed_b, jnp.pad(others, ((0, 14), (0, 0)))], axis=0)
     others = lax.all_gather(others, PLANE)
     grad_qkv, others = hold((grad_qkv, others))
-    grad_mixed_all = others[:, :tok].reshape(HEADS * tok, width)
+    grad_mixed_all = others.reshape(-1, width)
     others = jnp.sum(f32(others[:, tok : tok + 2]), axis=0).reshape(2, planes, HEADS, rows)
     others = lax.dynamic_index_in_dim(others, lax.axis_index(PLANE), 2, keepdims=False)
     others = jnp.swapaxes(others, 0, 1).reshape(planes, 1, 2 * rows)
     others = bf(jnp.pad(others, ((0, 0), (0, 7), (0, 2 * HEAD_DIM - 2 * rows))))
     grad_w = bf(mm_tn(normed_all, grad_qkv))
     grad_qkv, grad_w = hold((grad_qkv, grad_w))
-    sums = [core_sum(v.reshape(group, 4, rows, ff_own), grad_qkv) for v in grad_halves]
+    sums = [
+        core_sum(v.reshape(group, 4, rows, ff_own), late)
+        for v, late in zip(grad_halves, (grad_head, grad_qkv))
+    ]
     sums.append(core_sum(grad_down_w.reshape(1, 4, ff_own // 4, width), grad_qkv))
     grad_w = grad_w.reshape(planes, -1, 2 * HEAD_DIM)
     grad_out_w = bf(mm_tn(attn_cols, grad_mixed_all)).reshape(planes, -1, 2 * HEAD_DIM)

time: 769 us -> 752 us (0.978)
  matrix products: 128 us -> 115 us
  waiting for transfers between devices: 304 us -> 312 us
    all_to_all x8, waiting for transfers between devices: 92.3 us -> 45.7 us  [swap(): return lax.all_to_all(v, axes, split_axis=0, concat_axis=0, tiled=True)]
    all_gather x1, waiting for transfers between devices: 0.01 us -> 17.4 us  [ladder_shards(): lax.all_gather(out_line, PLANE, axis=1, tiled=False).reshape(q_width, width)]
    ppermute x6, waiting for transfers between devices: 0.33 us -> 16.7 us  [ring_gather(): behind = lax.ppermute(behind, LADDER, onward)]
    dot_general x21, matrix products: 128 us -> 115 us  [dot(): lax.dot_general(left, right, (dims, ((), ())), preferred_element_type=jnp...]
    ppermute x29, waiting for transfers between devices: 81.4 us -> 91 us  [flip(): return lax.ppermute(v, axis, [(0, 1), (1, 0)])]
    dynamic_update_slice x12, local copies, waits for them, and re-layouts: 23 us -> 14.3 us  [quad_place(): lax.dynamic_update_slice(whole, block[:, None], (0, me ^ bits, 0, part *...]
    unnamed x185 -> x194, local copies, waits for them, and re-layouts: 16.2 us -> 22.1 us
  transfers between devices with their start and end apart: 79 -> 79, of which waited for: 41 -> 44; matrix products, arithmetic and copies ran while one was open for 33% -> 33% of each run, Pallas kernels for 0% -> 0%
where the time goes in v1:
time: 752 us; the launch traced here: 743 us
  waiting for transfers between devices  312 us (41%)
  matrix products  115 us (15%)
  local copies, waits for them, and re-layouts  104 us (14%)
  starting transfers between devices  96.3 us (13%)
  other arithmetic  81.1 us (11%)
  between operations  18.6 us (2%)
  blocking collectives  16 us (2%)
    dot_general x21, matrix products, dot(): lax.dot_general(left, right, (dims, ((), ())), preferred_element_type=jnp...  115 us
    ppermute x29, waiting for transfers between devices, flip(): return lax.ppermute(v, axis, [(0, 1), (1, 0)])  91 us
    all_to_all x8, waiting for transfers between devices, swap(): return lax.all_to_all(v, axes, split_axis=0, concat_axis=0, tiled=True)  45.7 us
    ppermute x6, waiting for transfers between devices, ring_gather(): ahead = lax.ppermute(ahead, LADDER, back)  40.3 us
    ppermute x6, waiting for transfers between devices, ring_scatter(): ahead = lax.ppermute(to_ahead, LADDER, onward)  34.2 us
    all_to_all x8, starting transfers between devices, swap(): return lax.all_to_all(v, axes, split_axis=0, concat_axis=0, tiled=True)  32.6 us
    sub x5, other arithmetic, adam_step(): return (weight - rate * (ratio + decay * weight), first_new, second_new)  25.1 us
    convert_element_type x16, other arithmetic, bf(): return v.astype(jnp.bfloat16)  24.5 us
  transfers between devices with their start and end apart: 79, of which 44 were waited for; matrix products, arithmetic and copies ran while one was open for 33% of the time, Pallas kernels for 0%

profile of v1, /device:TPU:0, one launch (start us, length us, event | category | flops | bytes accessed | tf_op | source)
XLA Modules:
  0.0 743.1 jit_solution(6625396506361212487)
XLA Ops:
  12.6 16.0 %all_to_all.45 = bf16[8,80,512]{2,1,0:T(8,128)(2,1)} all-to-all(bf16[8,80,512]{2,1,0:T(8,128)(2,1)S(1)} %copy.162), channel_id=1, replica_groups=mesh['dh'=2,'dl'=2,'ctx'=2,'fy'=2,'core'=2] {'ctx','fy','core'}, dimensions={0} | all-to-all | bytes 1310720 | tf_op jit(solution)/shard_map/all_to_all | solution.py:98
  33.3 4.7 collective-permute-done.8
  44.3 7.3 collective-permute-done.12
  53.1 7.1 collective-permute-done.13
  66.0 6.5 copy.164
  80.2 9.5 %collective-permute-done.5 = bf16[128,2304]{1,0:T(8,128)(2,1)S(1)} collective-permute-done((bf16[128,2304]{1,0:T(8,128)(2,1)}, bf16[128,2304]{1,0:T(8,128)(2,1)S(1)}, u32[]{:S(2)}, u32[]{:S(2)}) %collective-permute-start.5) | collective-permute-done | bytes 589856 | tf_op jit(solution)/shard_map/ppermute | solution.py:106
  94.9 11.5 %all-gather.7.cloned.1.call-done = bf16[32,80,512]{2,1,0:T(8,128)(2,1)} async-done(((bf16[8,80,512]{2,1,0:T(8,128)(2,1)}), bf16[32,80,512]{2,1,0:T(8,128)(2,1)}) %all-gather.7.cloned.1.call-update) | async-done | bytes 2621456 | tf_op jit(solution)/shard_map/all_gather | solution.py:294
  133.9 9.5 %all-to-all-done.1 = bf16[8,72,1152]{2,1,0:T(8,128)(2,1)S(1)} async-done(((bf16[8,72,1152]{2,1,0:T(8,128)(2,1)}), bf16[8,72,1152]{2,1,0:T(8,128)(2,1)S(1)}, u32[]{:S(2)}, u32[]{:S(2)}) %all-to-all-start.1) | async-done | bytes 1327136 | tf_op jit(solution)/shard_map/all_to_all | solution.py:98
  151.1 12.0 %all-to-all-done.2 = bf16[8,128,256]{1,2,0:T(8,128)(2,1)S(1)} async-done(((bf16[8,128,256]{1,2,0:T(8,128)(2,1)}), bf16[8,128,256]{1,2,0:T(8,128)(2,1)S(1)}, u32[]{:S(2)}, u32[]{:S(2)}) %all-to-all-start.2) | async-done | bytes 524320 | tf_op jit(solution)/shard_map/all_to_all | solution.py:98
  172.3 4.6 broadcast_in_dim.130
  178.1 17.4 %all-gather.9.cloned.1.call-done = bf16[4,512,2304]{2,1,0:T(8,128)(2,1)} async-done(((bf16[4,64,2304]{2,1,0:T(8,128)(2,1)}), bf16[4,512,2304]{2,1,0:T(8,128)(2,1)}) %all-gather.9.cloned.1.call-update) | async-done | bytes 9437200 | tf_op jit(solution)/shard_map/all_gather | solution.py:304
  195.6 5.2 multiply_reduce_fusion.6
  212.4 8.2 %collective-permute-done.15 = bf16[128,2304]{1,0:T(8,128)(2,1)S(1)} collective-permute-done((bf16[128,2304]{1,0:T(8,128)(2,1)}, bf16[128,2304]{1,0:T(8,128)(2,1)S(1)}, u32[]{:S(2)}, u32[]{:S(2)}) %collective-permute-start.15) | collective-permute-done | bytes 589856 | tf_op jit(solution)/shard_map/ppermute | solution.py:164
  224.8 13.0 %collective-permute-done.16 = bf16[128,2304]{1,0:T(8,128)(2,1)S(1)} collective-permute-done((bf16[128,2304]{1,0:T(8,128)(2,1)S(1)}, bf16[128,2304]{1,0:T(8,128)(2,1)S(1)}, u32[]{:S(2)}, u32[]{:S(2)}) %collective-permute-start.16) | collective-permute-done | bytes 589856 | tf_op jit(solution)/shard_map/ppermute | solution.py:163
  249.3 5.7 collective-permute-done.19
  260.7 6.3 collective-permute-done.20
  270.4 13.5 %fusion.141 = f32[1024,2304]{1,0:T(8,128)S(1)} fusion(bf16[1024,2304]{1,0:T(8,128)(2,1)S(1)} %constant_dynamic-update-slice_fusion, bf16[2304,2304]{1,0:T(8,128)(2,1)} %bitcast.50), kind=kOutput, calls=%fused_computation.353 | convolution fusion | flops 10871635968 | bytes 24772608 | tf_op jit(solution)/shard_map/dot_general | solution.py:38
  287.7 6.5 convolution_convert_fusion.4
  296.9 7.0 collective-permute-done.32
  308.4 12.7 %collective-permute-done.33 = bf16[128,2304]{1,0:T(8,128)(2,1)S(1)} collective-permute-done((bf16[128,2304]{1,0:T(8,128)(2,1)S(1)}, bf16[128,2304]{1,0:T(8,128)(2,1)S(1)}, u32[]{:S(2)}, u32[]{:S(2)}) %collective-permute-start.33) | collective-permute-done | bytes 589856 | tf_op jit(solution)/shard_map/ppermute | solution.py:207
  323.8 11.8 %collective-permute-done.35 = bf16[128,2304]{1,0:T(8,128)(2,1)S(1)} collective-permute-done((bf16[128,2304]{1,0:T(8,128)(2,1)S(1)}, bf16[128,2304]{1,0:T(8,128)(2,1)S(1)}, u32[]{:S(2)}, u32[]{:S(2)}) %collective-permute-start.35) | collective-permute-done | bytes 589856 | tf_op jit(solution)/shard_map/ppermute | solution.py:207
  342.9 12.7 %all-to-all-done.4 = bf16[8,128,256]{1,2,0:T(8,128)(2,1)S(1)} async-done(((bf16[8,128,256]{1,2,0:T(8,128)(2,1)}), bf16[8,128,256]{1,2,0:T(8,128)(2,1)S(1)}, u32[]{:S(2)}, u32[]{:S(2)}) %all-to-all-start.4) | async-done | bytes 524320 | tf_op jit(solution)/shard_map/all_to_all | solution.py:98
  364.1 12.3 %collective-permute-done.40 = bf16[128,2304]{1,0:T(8,128)(2,1)S(1)} collective-permute-done((bf16[128,2304]{1,0:T(8,128)(2,1)S(1)}, bf16[128,2304]{1,0:T(8,128)(2,1)S(1)}, u32[]{:S(2)}, u32[]{:S(2)}) %collective-permute-start.40) | collective-permute-done | bytes 589856 | tf_op jit(solution)/shard_map/ppermute | solution.py:164
  378.6 11.3 %collective-permute-done.42 = bf16[128,2304]{1,0:T(8,128)(2,1)S(1)} collective-permute-done((bf16[128,2304]{1,0:T(8,128)(2,1)S(1)}, bf16[128,2304]{1,0:T(8,128)(2,1)S(1)}, u32[]{:S(2)}, u32[]{:S(2)}) %collective-permute-start.42) | collective-permute-done | bytes 589856 | tf_op jit(solution)/shard_map/ppermute | solution.py:164
  392.0 8.3 %fusion.30 = (bf16[640,1152]{1,0:T(8,128)(2,1)S(1)}, bf16[640,1152]{1,0:T(8,128)(2,1)S(1)}) fusion(f32[1024,2304]{1,0:T(8,128)} %copy-done.7, bf16[640,2304]{1,0:T(8,128)(2,1)S(1)} %constant_dynamic-update-slice_fusion.9, bf16[1152,2304]{1,0:T(8,128)(2,1)S(1)} %bitcast.310), kind=kOutput, calls=%fused_computation.63 | convolution fusion | flops 3415080960 | bytes 17104896 | tf_op jit(solution)/shard_map/dot_general | solution.py:38
  406.3 10.5 %convolution_convert_fusion.5 = bf16[640,2304]{1,0:T(8,128)(2,1)S(1)} fusion(bf16[640,2304]{1,0:T(8,128)(2,1)S(1)} %pad_maximum_fusion, bf16[2304,2304]{1,0:T(8,128)(2,1)} %bitcast.50), kind=kOutput, calls=%fused_computation.26 | convolution fusion | flops 6796247040 | bytes 16515072 | tf_op jit(solution)/shard_map/dot_general | solution.py:38
  418.1 5.9 fusion.43
  424.2 8.3 %convolution_convert_fusion.7 = bf16[384,2304]{1,0:T(8,128)(2,1)S(1)} fusion(bf16[384,2304]{1,0:T(8,128)(2,1)S(1)} %pad_maximum_fusion.2, bf16[2304,2304]{1,0:T(8,128)(2,1)} %bitcast.50), kind=kOutput, calls=%fused_computation.44 | convolution fusion | flops 4077748224 | bytes 14155776 | tf_op jit(solution)/shard_map/dot_general | solution.py:38
  435.2 5.0 collective-permute-done.48
  446.8 8.0 %convolution_convert_fusion.1 = bf16[2304,1152]{1,0:T(8,128)(2,1)} fusion(bf16[1024,2304]{1,0:T(8,128)(2,1)S(1)} %bitcast.335, bf16[1024,2304]{1,0:T(8,128)(2,1)S(1)} %constant_dynamic-update-slice_fusion.18), kind=kOutput, calls=%fused_computation.1 | convolution fusion | flops 5438472192 | bytes 12386304 | tf_op jit(solution)/shard_map/dot_general | solution.py:38
  461.9 8.0 %convolution_convert_fusion.2 = bf16[2304,1152]{1,0:T(8,128)(2,1)} fusion(bf16[1024,2304]{1,0:T(8,128)(2,1)S(1)} %bitcast.335, bf16[1024,2304]{1,0:T(8,128)(2,1)S(1)} %constant_dynamic-update-slice_fusion.18), kind=kOutput, calls=%fused_computation.2 | convolution fusion | flops 5438472192 | bytes 12386304 | tf_op jit(solution)/shard_map/dot_general | solution.py:38
  469.9 5.4 collective-permute-done.51
  479.5 7.5 %convolution_convert_fusion = bf16[1152,2304]{1,0:T(8,128)(2,1)} fusion(bf16[1024,1152]{1,0:T(8,128)(2,1)S(1)} %copy-done.26, bf16[384,2304]{1,0:T(8,128)(2,1)S(1)} %copy-done.46, bf16[640,2304]{1,0:T(8,128)(2,1)S(1)} %copy-done.52), kind=kOutput, calls=%fused_computation | convolution fusion | flops 5447909376 | bytes 12386304 | tf_op jit(solution)/shard_map/dot_general | solution.py:38
  492.7 5.9 dynamic-slice_bitcast_fusion.2
  498.6 5.7 dynamic-slice_bitcast_fusion
  508.8 4.4 all-to-all-start.5
  513.2 5.3 dynamic-slice_bitcast_fusion.4
  518.8 8.7 %all-to-all-done.5 = bf16[8,128,256]{1,2,0:T(8,128)(2,1)} async-done(((bf16[8,128,256]{1,2,0:T(8,128)(2,1)}), bf16[8,128,256]{1,2,0:T(8,128)(2,1)}, u32[]{:S(2)}, u32[]{:S(2)}) %all-to-all-start.5) | async-done | bytes 524320 | tf_op jit(solution)/shard_map/all_to_all | solution.py:98
  529.0 4.7 multiply_convert_fusion
  548.7 23.0 %collective-permute-done.60 = bf16[8,72,1152]{2,1,0:T(8,128)(2,1)S(1)} collective-permute-done((bf16[8,72,1152]{2,1,0:T(8,128)(2,1)S(1)}, bf16[8,72,1152]{2,1,0:T(8,128)(2,1)S(1)}, u32[]{:S(2)}, u32[]{:S(2)}) %collective-permute-start.60) | collective-permute-done | bytes 1327136 | tf_op jit(solution)/shard_map/ppermute | solution.py:106
  577.9 6.7 convolution_convert_fusion.6
  585.9 5.3 convolution_convert_fusion.8
  615.1 18.7 %collective-permute-done.58 = bf16[8,72,1152]{2,1,0:T(8,128)(2,1)} collective-permute-done((bf16[8,72,1152]{2,1,0:T(8,128)(2,1)}, bf16[8,72,1152]{2,1,0:T(8,128)(2,1)}, u32[]{:S(2)}, u32[]{:S(2)}) %collective-permute-start.58) | collective-permute-done | bytes 1327136 | tf_op jit(solution)/shard_map/ppermute | solution.py:106
  649.1 4.8 all-to-all-start.7
  654.0 16.9 %collective-permute-done.66 = bf16[1,288,2304]{2,1,0:T(8,128)(2,1)} collective-permute-done((bf16[1,288,2304]{2,1,0:T(8,128)(2,1)}, bf16[1,288,2304]{2,1,0:T(8,128)(2,1)}, u32[]{:S(2)}, u32[]{:S(2)}) %collective-permute-start.66) | collective-permute-done | bytes 1327136 | tf_op jit(solution)/shard_map/ppermute | solution.py:106
  678.3 7.8 %convert_subtract_fusion.1 = (f32[288,2304]{1,0:T(8,128)}, f32[288,2304]{1,0:T(8,128)}, f32[288,2304]{1,0:T(8,128)}) fusion(bf16[288,2304]{1,0:T(8,128)(2,1)S(1)} %copy-done.12, bf16[1,288,2304]{2,1,0:T(8,128)(2,1)} %collective-permute-done.66, bf16[1,288,2304]{2,1,0:T(8,128)(2,1)S(1)} %copy-done.14, f32[288,2304]{1,0:T(8,128)} %param.32, f32[288,2304]{1,0:T(8,128)} %param.33), kind=kLoop, calls=%fused_computation.55 | loop fusion | flops 13934592 | bytes 17252352 | tf_op jit(solution)/shard_map/sub | solution.py:86
  688.4 7.6 %collective-permute-done.63 = bf16[128,2304]{1,0:T(8,128)(2,1)S(1)} collective-permute-done((bf16[128,2304]{1,0:T(8,128)(2,1)S(1)}, bf16[128,2304]{1,0:T(8,128)(2,1)S(1)}, u32[]{:S(2)}, u32[]{:S(2)}) %collective-permute-start.63) | collective-permute-done | bytes 589856 | tf_op jit(solution)/shard_map/ppermute | solution.py:106
  716.5 12.5 %convert_subtract_fusion = (f32[72,18432]{1,0:T(8,128)}, f32[72,18432]{1,0:T(8,128)}, f32[72,18432]{1,0:T(8,128)}, f32[72]{0:T(128)S(1)}) fusion(bf16[72,18432]{1,0:T(8,128)(2,1)S(1)} %copy-done.6, bf16[72,9216]{1,0:T(8,128)(2,1)} %bitcast.303, bf16[72,9216]{1,0:T(8,128)(2,1)S(1)} %bitcast.302, f32[72,18432]{1,0:T(8,128)} %param.30, f32[72,18432]{1,0:T(8,128)} %param.31), kind=kLoop, calls=%fused_computation.11 | loop fusion | flops 29196216 | bytes 31850784 | tf_op jit(solution)/shard_map/sub | solution.py:86
  (491 shorter events, 287.0 us)
Async XLA Ops:
  7.2 99.1 %all-gather.7.cloned.1.call-start = ((), (), s32[]{:S(2)}) async-start(), calls=%async_computation.11 | async-start | bytes 3276800 | tf_op jit(solution)/shard_map/all_gather | solution.py:294
  44.2 151.4 %all-gather.9.cloned.1.call-start = ((), (), s32[]{:S(2)}) async-start(), calls=%async_computation.12 | async-start | bytes 10616832 | tf_op jit(solution)/shard_map/all_gather | solution.py:304
  107.5 35.9 %all-to-all-start.1 = ((bf16[8,72,1152]{2,1,0:T(8,128)(2,1)}), bf16[8,72,1152]{2,1,0:T(8,128)(2,1)S(1)}, u32[]{:S(2)}, u32[]{:S(2)}) async-start(bf16[8,72,1152]{2,1,0:T(8,128)(2,1)} %copy.163), calls=%async_computation.1 | async-start | bytes 2654208 | tf_op jit(solution)/shard_map/all_to_all | solution.py:98
  144.7 18.4 %all-to-all-start.2 = ((bf16[8,128,256]{1,2,0:T(8,128)(2,1)}), bf16[8,128,256]{1,2,0:T(8,128)(2,1)S(1)}, u32[]{:S(2)}, u32[]{:S(2)}) async-start(bf16[8,128,256]{1,2,0:T(8,128)(2,1)} %copy_bitcast_fusion.2), calls=%async_computation.2 | async-start | bytes 1048576 | tf_op jit(solution)/shard_map/all_to_all | solution.py:98
  163.1 46.2 %collective-permute-start.23 = (bf16[8,72,1152]{2,1,0:T(8,128)(2,1)}, bf16[8,72,1152]{2,1,0:T(8,128)(2,1)}, u32[]{:S(2)}, u32[]{:S(2)}) collective-permute-start(bf16[8,72,1152]{2,1,0:T(8,128)(2,1)} %copy-done.16), channel_id=1, source_target_pairs={{0,2},{2,0},{1,3},{3,1},{4,6},{6,4},{5,7},{7,5},{8,10},{10,8},{9,1... | collective-permute-start | bytes 3981320 | tf_op jit(solution)/shard_map/ppermute | solution.py:106
  164.6 42.1 %collective-permute-start.22 = (bf16[8,72,1152]{2,1,0:T(8,128)(2,1)}, bf16[8,72,1152]{2,1,0:T(8,128)(2,1)}, u32[]{:S(2)}, u32[]{:S(2)}) collective-permute-start(bf16[8,72,1152]{2,1,0:T(8,128)(2,1)} %copy-done.16), channel_id=1, source_target_pairs={{0,1},{1,0},{2,3},{3,2},{4,5},{5,4},{6,7},{7,6},{8,9},{9,8},{10,11... | collective-permute-start | bytes 3981320 | tf_op jit(solution)/shard_map/ppermute | solution.py:106
  167.2 42.1 %all-to-all-start.3 = ((bf16[8,72,1152]{2,1,0:T(8,128)(2,1)}), bf16[8,72,1152]{2,1,0:T(8,128)(2,1)}, u32[]{:S(2)}, u32[]{:S(2)}) async-start(bf16[8,72,1152]{2,1,0:T(8,128)(2,1)} %copy.168), calls=%async_computation.3 | async-start | bytes 2654208 | tf_op jit(solution)/shard_map/all_to_all | solution.py:98
  202.6 18.0 %collective-permute-start.15 = (bf16[128,2304]{1,0:T(8,128)(2,1)}, bf16[128,2304]{1,0:T(8,128)(2,1)S(1)}, u32[]{:S(2)}, u32[]{:S(2)}) collective-permute-start(bf16[128,2304]{1,0:T(8,128)(2,1)} %get-tuple-element.170), channel_id=1, source_target_pairs={{8,0},{16,8},{24,16},{28,24},{20,28},{12,20},{4,12},{0,4},{9,1},{1... | collective-permute-start | bytes 1769480 | tf_op jit(solution)/shard_map/ppermute | solution.py:164
  205.1 17.8 %collective-permute-start.14 = (bf16[128,2304]{1,0:T(8,128)(2,1)}, bf16[128,2304]{1,0:T(8,128)(2,1)S(1)}, u32[]{:S(2)}, u32[]{:S(2)}) collective-permute-start(bf16[128,2304]{1,0:T(8,128)(2,1)} %get-tuple-element.170), channel_id=1, source_target_pairs={{0,8},{8,16},{16,24},{24,28},{28,20},{20,12},{12,4},{4,0},{1,9},{9... | collective-permute-start | bytes 1769480 | tf_op jit(solution)/shard_map/ppermute | solution.py:163
  209.2 37.4 %collective-permute-start.26 = (bf16[8,72,1152]{2,1,0:T(8,128)(2,1)}, bf16[8,72,1152]{2,1,0:T(8,128)(2,1)S(1)}, u32[]{:S(2)}, u32[]{:S(2)}) collective-permute-start(bf16[8,72,1152]{2,1,0:T(8,128)(2,1)} %all-to-all-done.3), channel_id=1, source_target_pairs={{0,2},{2,0},{1,3},{3,1},{4,6},{6,4},{5,7},{7,5},{8,10},{10,8},{9,1... | collective-permute-start | bytes 3981320 | tf_op jit(solution)/shard_map/ppermute | solution.py:106
  209.2 37.7 %collective-permute-start.25 = (bf16[8,72,1152]{2,1,0:T(8,128)(2,1)}, bf16[8,72,1152]{2,1,0:T(8,128)(2,1)S(1)}, u32[]{:S(2)}, u32[]{:S(2)}) collective-permute-start(bf16[8,72,1152]{2,1,0:T(8,128)(2,1)} %all-to-all-done.3), channel_id=1, source_target_pairs={{0,1},{1,0},{2,3},{3,2},{4,5},{5,4},{6,7},{7,6},{8,9},{9,8},{10,11... | collective-permute-start | bytes 3981320 | tf_op jit(solution)/shard_map/ppermute | solution.py:106
  209.3 31.7 %collective-permute-start.24 = (bf16[8,72,1152]{2,1,0:T(8,128)(2,1)}, bf16[8,72,1152]{2,1,0:T(8,128)(2,1)S(1)}, u32[]{:S(2)}, u32[]{:S(2)}) collective-permute-start(bf16[8,72,1152]{2,1,0:T(8,128)(2,1)} %collective-permute-done.23), channel_id=1, source_target_pairs={{0,1},{1,0},{2,3},{3,2},{4,5},{5,4},{6,7},{7,6},{8,9},{9,8},{10,11... | collective-permute-start | bytes 3981320 | tf_op jit(solution)/shard_map/ppermute | solution.py:106
  220.6 18.6 %collective-permute-start.17 = (bf16[128,2304]{1,0:T(8,128)(2,1)S(1)}, bf16[128,2304]{1,0:T(8,128)(2,1)S(1)}, u32[]{:S(2)}, u32[]{:S(2)}) collective-permute-start(bf16[128,2304]{1,0:T(8,128)(2,1)S(1)} %collective-permute-done.15), channel_id=1, source_target_pairs={{8,0},{16,8},{24,16},{28,24},{20,28},{12,20},{4,12},{0,4},{9,1},{1... | collective-permute-start | bytes 1769480 | tf_op jit(solution)/shard_map/ppermute | solution.py:164
  222.9 14.8 %collective-permute-start.16 = (bf16[128,2304]{1,0:T(8,128)(2,1)S(1)}, bf16[128,2304]{1,0:T(8,128)(2,1)S(1)}, u32[]{:S(2)}, u32[]{:S(2)}) collective-permute-start(bf16[128,2304]{1,0:T(8,128)(2,1)S(1)} %collective-permute-done.14), channel_id=1, source_target_pairs={{0,8},{8,16},{16,24},{24,28},{28,20},{20,12},{12,4},{4,0},{1,9},{9... | collective-permute-start | bytes 1769480 | tf_op jit(solution)/shard_map/ppermute | solution.py:163
  237.8 31.1 %collective-permute-start.29 = (bf16[1,288,2304]{2,1,0:T(8,128)(2,1)S(1)}, bf16[1,288,2304]{2,1,0:T(8,128)(2,1)S(1)}, u32[]{:S(2)}, u32[]{:S(2)}) collective-permute-start(bf16[1,288,2304]{2,1,0:T(8,128)(2,1)S(1)} %bitcast.300), channel_id=1, source_target_pairs={{0,2},{2,0},{1,3},{3,1},{4,6},{6,4},{5,7},{7,5},{8,10},{10,8},{9,1... | collective-permute-start | bytes 3981320 | tf_op jit(solution)/shard_map/ppermute | solution.py:106
  239.1 29.7 %collective-permute-start.28 = (bf16[1,288,2304]{2,1,0:T(8,128)(2,1)S(1)}, bf16[1,288,2304]{2,1,0:T(8,128)(2,1)S(1)}, u32[]{:S(2)}, u32[]{:S(2)}) collective-permute-start(bf16[1,288,2304]{2,1,0:T(8,128)(2,1)S(1)} %bitcast.301), channel_id=1, source_target_pairs={{0,1},{1,0},{2,3},{3,2},{4,5},{5,4},{6,7},{7,6},{8,9},{9,8},{10,11... | collective-permute-start | bytes 3981320 | tf_op jit(solution)/shard_map/ppermute | solution.py:106
  241.0 14.0 %collective-permute-start.19 = (bf16[128,2304]{1,0:T(8,128)(2,1)S(1)}, bf16[128,2304]{1,0:T(8,128)(2,1)S(1)}, u32[]{:S(2)}, u32[]{:S(2)}) collective-permute-start(bf16[128,2304]{1,0:T(8,128)(2,1)S(1)} %collective-permute-done.17), channel_id=1, source_target_pairs={{8,0},{16,8},{24,16},{28,24},{20,28},{12,20},{4,12},{0,4},{9,1},{1... | collective-permute-start | bytes 1769480 | tf_op jit(solution)/shard_map/ppermute | solution.py:164
  246.9 22.3 %collective-permute-start.27 = (bf16[8,72,1152]{2,1,0:T(8,128)(2,1)S(1)}, bf16[8,72,1152]{2,1,0:T(8,128)(2,1)S(1)}, u32[]{:S(2)}, u32[]{:S(2)}) collective-permute-start(bf16[8,72,1152]{2,1,0:T(8,128)(2,1)S(1)} %collective-permute-done.26), channel_id=1, source_target_pairs={{0,1},{1,0},{2,3},{3,2},{4,5},{5,4},{6,7},{7,6},{8,9},{9,8},{10,11... | collective-permute-start | bytes 3981320 | tf_op jit(solution)/shard_map/ppermute | solution.py:106
  268.9 18.7 %collective-permute-start.30 = (bf16[1,288,2304]{2,1,0:T(8,128)(2,1)S(1)}, bf16[1,288,2304]{2,1,0:T(8,128)(2,1)S(1)}, u32[]{:S(2)}, u32[]{:S(2)}) collective-permute-start(bf16[1,288,2304]{2,1,0:T(8,128)(2,1)S(1)} %collective-permute-done.29), channel_id=1, source_target_pairs={{0,1},{1,0},{2,3},{3,2},{4,5},{5,4},{6,7},{7,6},{8,9},{9,8},{10,11... | collective-permute-start | bytes 3981320 | tf_op jit(solution)/shard_map/ppermute | solution.py:106
  306.3 14.8 %collective-permute-start.33 = (bf16[128,2304]{1,0:T(8,128)(2,1)S(1)}, bf16[128,2304]{1,0:T(8,128)(2,1)S(1)}, u32[]{:S(2)}, u32[]{:S(2)}) collective-permute-start(bf16[128,2304]{1,0:T(8,128)(2,1)S(1)} %get-tuple-element.92), channel_id=1, source_target_pairs={{0,8},{8,16},{16,24},{24,28},{28,20},{20,12},{12,4},{4,0},{1,9},{9... | collective-permute-start | bytes 1769480 | tf_op jit(solution)/shard_map/ppermute | solution.py:207
  306.7 14.8 %collective-permute-start.34 = (bf16[128,2304]{1,0:T(8,128)(2,1)S(1)}, bf16[128,2304]{1,0:T(8,128)(2,1)S(1)}, u32[]{:S(2)}, u32[]{:S(2)}) collective-permute-start(bf16[128,2304]{1,0:T(8,128)(2,1)S(1)} %get-tuple-element.93), channel_id=1, source_target_pairs={{8,0},{16,8},{24,16},{28,24},{20,28},{12,20},{4,12},{0,4},{9,1},{1... | collective-permute-start | bytes 1769480 | tf_op jit(solution)/shard_map/ppermute | solution.py:208
  321.7 13.9 %collective-permute-start.35 = (bf16[128,2304]{1,0:T(8,128)(2,1)S(1)}, bf16[128,2304]{1,0:T(8,128)(2,1)S(1)}, u32[]{:S(2)}, u32[]{:S(2)}) collective-permute-start(bf16[128,2304]{1,0:T(8,128)(2,1)S(1)} %get-tuple-element.94), channel_id=1, source_target_pairs={{0,8},{8,16},{16,24},{24,28},{28,20},{20,12},{12,4},{4,0},{1,9},{9... | collective-permute-start | bytes 1769480 | tf_op jit(solution)/shard_map/ppermute | solution.py:207
  337.3 20.6 %collective-permute-start.37 = (bf16[128,2304]{1,0:T(8,128)(2,1)}, bf16[128,2304]{1,0:T(8,128)(2,1)}, u32[]{:S(2)}, u32[]{:S(2)}) collective-permute-start(bf16[128,2304]{1,0:T(8,128)(2,1)} %get-tuple-element.96), channel_id=1, source_target_pairs={{0,8},{8,16},{16,24},{24,28},{28,20},{20,12},{12,4},{4,0},{1,9},{9... | collective-permute-start | bytes 1769480 | tf_op jit(solution)/shard_map/ppermute | solution.py:207
  338.7 19.1 %collective-permute-start.38 = (bf16[128,2304]{1,0:T(8,128)(2,1)}, bf16[128,2304]{1,0:T(8,128)(2,1)}, u32[]{:S(2)}, u32[]{:S(2)}) collective-permute-start(bf16[128,2304]{1,0:T(8,128)(2,1)} %get-tuple-element.97), channel_id=1, source_target_pairs={{8,0},{16,8},{24,16},{28,24},{20,28},{12,20},{4,12},{0,4},{9,1},{1... | collective-permute-start | bytes 1769480 | tf_op jit(solution)/shard_map/ppermute | solution.py:208
  339.3 16.4 %all-to-all-start.4 = ((bf16[8,128,256]{1,2,0:T(8,128)(2,1)}), bf16[8,128,256]{1,2,0:T(8,128)(2,1)S(1)}, u32[]{:S(2)}, u32[]{:S(2)}) async-start(bf16[8,128,256]{1,2,0:T(8,128)(2,1)} %bitcast.38), calls=%async_computation.4 | async-start | bytes 1048576 | tf_op jit(solution)/shard_map/all_to_all | solution.py:98
  342.8 235.1 %all-gather.11.cloned.1.call-start = ((), (), s32[]{:S(2)}) async-start(), calls=%async_computation.13 | async-start | bytes 5971968 | tf_op jit(solution)/shard_map/all_gather | solution.py:397
  361.6 14.8 %collective-permute-start.40 = (bf16[128,2304]{1,0:T(8,128)(2,1)S(1)}, bf16[128,2304]{1,0:T(8,128)(2,1)S(1)}, u32[]{:S(2)}, u32[]{:S(2)}) collective-permute-start(bf16[128,2304]{1,0:T(8,128)(2,1)S(1)} %get-tuple-element.168), channel_id=1, source_target_pairs={{8,0},{16,8},{24,16},{28,24},{20,28},{12,20},{4,12},{0,4},{9,1},{1... | collective-permute-start | bytes 1769480 | tf_op jit(solution)/shard_map/ppermute | solution.py:164
  363.8 14.4 %collective-permute-start.39 = (bf16[128,2304]{1,0:T(8,128)(2,1)S(1)}, bf16[128,2304]{1,0:T(8,128)(2,1)S(1)}, u32[]{:S(2)}, u32[]{:S(2)}) collective-permute-start(bf16[128,2304]{1,0:T(8,128)(2,1)S(1)} %get-tuple-element.168), channel_id=1, source_target_pairs={{0,8},{8,16},{16,24},{24,28},{28,20},{20,12},{12,4},{4,0},{1,9},{9... | collective-permute-start | bytes 1769480 | tf_op jit(solution)/shard_map/ppermute | solution.py:163
  403.3 14.7 %collective-permute-start.46 = (bf16[64,2304]{1,0:T(8,128)(2,1)S(1)}, bf16[64,2304]{1,0:T(8,128)(2,1)S(1)}, u32[]{:S(2)}, u32[]{:S(2)}) collective-permute-start(bf16[64,2304]{1,0:T(8,128)(2,1)S(1)} %slice.392), channel_id=1, source_target_pairs={{8,0},{16,8},{24,16},{28,24},{20,28},{12,20},{4,12},{0,4},{9,1},{1... | collective-permute-start | bytes 884744 | tf_op jit(solution)/shard_map/ppermute | solution.py:169
  444.7 14.4 %collective-permute-start.49 = (bf16[128,2304]{1,0:T(8,128)(2,1)S(1)}, bf16[128,2304]{1,0:T(8,128)(2,1)S(1)}, u32[]{:S(2)}, u32[]{:S(2)}) collective-permute-start(bf16[128,2304]{1,0:T(8,128)(2,1)S(1)} %pad_maximum_fusion.8), channel_id=1, source_target_pairs={{0,8},{8,16},{16,24},{24,28},{28,20},{20,12},{12,4},{4,0},{1,9},{9... | collective-permute-start | bytes 1769480 | tf_op jit(solution)/shard_map/ppermute | solution.py:207
  444.8 14.3 %collective-permute-start.50 = (bf16[128,2304]{1,0:T(8,128)(2,1)S(1)}, bf16[128,2304]{1,0:T(8,128)(2,1)S(1)}, u32[]{:S(2)}, u32[]{:S(2)}) collective-permute-start(bf16[128,2304]{1,0:T(8,128)(2,1)S(1)} %pad_maximum_fusion.9), channel_id=1, source_target_pairs={{8,0},{16,8},{24,16},{28,24},{20,28},{12,20},{4,12},{0,4},{9,1},{1... | collective-permute-start | bytes 1769480 | tf_op jit(solution)/shard_map/ppermute | solution.py:208
  459.4 15.9 %collective-permute-start.51 = (bf16[128,2304]{1,0:T(8,128)(2,1)S(1)}, bf16[128,2304]{1,0:T(8,128)(2,1)S(1)}, u32[]{:S(2)}, u32[]{:S(2)}) collective-permute-start(bf16[128,2304]{1,0:T(8,128)(2,1)S(1)} %get-tuple-element.106), channel_id=1, source_target_pairs={{0,8},{8,16},{16,24},{24,28},{28,20},{20,12},{12,4},{4,0},{1,9},{9... | collective-permute-start | bytes 1769480 | tf_op jit(solution)/shard_map/ppermute | solution.py:207
  461.0 15.7 %collective-permute-start.52 = (bf16[128,2304]{1,0:T(8,128)(2,1)S(1)}, bf16[128,2304]{1,0:T(8,128)(2,1)S(1)}, u32[]{:S(2)}, u32[]{:S(2)}) collective-permute-start(bf16[128,2304]{1,0:T(8,128)(2,1)S(1)} %get-tuple-element.107), channel_id=1, source_target_pairs={{8,0},{16,8},{24,16},{28,24},{20,28},{12,20},{4,12},{0,4},{9,1},{1... | collective-permute-start | bytes 1769480 | tf_op jit(solution)/shard_map/ppermute | solution.py:208
  498.6 95.8 %collective-permute-start.57 = (bf16[8,2,72,1152]{3,2,1,0:T(8,128)(2,1)}, bf16[8,2,72,1152]{3,2,1,0:T(8,128)(2,1)}, u32[]{:S(2)}, u32[]{:S(2)}) collective-permute-start(bf16[8,2,72,1152]{3,2,1,0:T(8,128)(2,1)} %get-tuple-element.180), channel_id=1, source_target_pairs={{0,1},{1,0},{2,3},{3,2},{4,5},{5,4},{6,7},{7,6},{8,9},{9,8},{10,11... | collective-permute-start | bytes 7962632 | tf_op jit(solution)/shard_map/ppermute | solution.py:106
  504.3 33.1 %collective-permute-start.59 = (bf16[8,2,72,1152]{3,2,1,0:T(8,128)(2,1)}, bf16[8,2,72,1152]{3,2,1,0:T(8,128)(2,1)}, u32[]{:S(2)}, u32[]{:S(2)}) collective-permute-start(bf16[8,2,72,1152]{3,2,1,0:T(8,128)(2,1)} %get-tuple-element.178), channel_id=1, source_target_pairs={{0,1},{1,0},{2,3},{3,2},{4,5},{5,4},{6,7},{7,6},{8,9},{9,8},{10,11... | collective-permute-start | bytes 7962632 | tf_op jit(solution)/shard_map/ppermute | solution.py:106
  508.8 18.7 %all-to-all-start.5 = ((bf16[8,128,256]{1,2,0:T(8,128)(2,1)}), bf16[8,128,256]{1,2,0:T(8,128)(2,1)}, u32[]{:S(2)}, u32[]{:S(2)}) async-start(bf16[8,128,256]{1,2,0:T(8,128)(2,1)} %bitcast.62), calls=%async_computation.5 | async-start | bytes 1048576 | tf_op jit(solution)/shard_map/all_to_all | solution.py:98
  518.5 92.7 %collective-permute-start.56 = (bf16[1,2,288,2304]{3,2,1,0:T(8,128)(2,1)}, bf16[1,2,288,2304]{3,2,1,0:T(8,128)(2,1)}, u32[]{:S(2)}, u32[]{:S(2)}) collective-permute-start(bf16[1,2,288,2304]{3,2,1,0:T(8,128)(2,1)} %get-tuple-element.182), channel_id=1, source_target_pairs={{0,1},{1,0},{2,3},{3,2},{4,5},{5,4},{6,7},{7,6},{8,9},{9,8},{10,11... | collective-permute-start | bytes 7962632 | tf_op jit(solution)/shard_map/ppermute | solution.py:106
  540.2 31.6 %collective-permute-start.60 = (bf16[8,72,1152]{2,1,0:T(8,128)(2,1)S(1)}, bf16[8,72,1152]{2,1,0:T(8,128)(2,1)S(1)}, u32[]{:S(2)}, u32[]{:S(2)}) collective-permute-start(bf16[8,72,1152]{2,1,0:T(8,128)(2,1)S(1)} %get-tuple-element.202), channel_id=1, source_target_pairs={{0,2},{2,0},{1,3},{3,1},{4,6},{6,4},{5,7},{7,5},{8,10},{10,8},{9,1... | collective-permute-start | bytes 3981320 | tf_op jit(solution)/shard_map/ppermute | solution.py:106
  573.2 41.9 %all-to-all-start.6 = ((bf16[8,72,1152]{2,1,0:T(8,128)(2,1)}), bf16[8,72,1152]{2,1,0:T(8,128)(2,1)}, u32[]{:S(2)}, u32[]{:S(2)}) async-start(bf16[8,72,1152]{2,1,0:T(8,128)(2,1)} %add_convert_fusion.5), calls=%async_computation.7 | async-start | bytes 2654208 | tf_op jit(solution)/shard_map/all_to_all | solution.py:98
  577.5 121.7 %reduce-scatter.2.cloned.1.call-start = ((), (), s32[]{:S(2)}) async-start(), calls=%async_computation.10 | async-start | bytes 4464640 | tf_op jit(solution)/shard_map/reduce_scatter | solution.py:94
  602.8 31.0 %collective-permute-start.58 = (bf16[8,72,1152]{2,1,0:T(8,128)(2,1)}, bf16[8,72,1152]{2,1,0:T(8,128)(2,1)}, u32[]{:S(2)}, u32[]{:S(2)}) collective-permute-start(bf16[8,72,1152]{2,1,0:T(8,128)(2,1)} %get-tuple-element.204), channel_id=1, source_target_pairs={{0,2},{2,0},{1,3},{3,1},{4,6},{6,4},{5,7},{7,5},{8,10},{10,8},{9,1... | collective-permute-start | bytes 3981320 | tf_op jit(solution)/shard_map/ppermute | solution.py:106
  611.1 29.1 %collective-permute-start.61 = (bf16[4,128,2304]{2,1,0:T(8,128)(2,1)}, bf16[4,128,2304]{2,1,0:T(8,128)(2,1)}, u32[]{:S(2)}, u32[]{:S(2)}) collective-permute-start(bf16[4,128,2304]{2,1,0:T(8,128)(2,1)} %dynamic-slice_bitcast_fusion.6), channel_id=1, source_target_pairs={{0,1},{1,0},{2,3},{3,2},{4,5},{5,4},{6,7},{7,6},{8,9},{9,8},{10,11... | collective-permute-start | bytes 7077896 | tf_op jit(solution)/shard_map/ppermute | solution.py:106
  638.6 32.4 %collective-permute-start.66 = (bf16[1,288,2304]{2,1,0:T(8,128)(2,1)}, bf16[1,288,2304]{2,1,0:T(8,128)(2,1)}, u32[]{:S(2)}, u32[]{:S(2)}) collective-permute-start(bf16[1,288,2304]{2,1,0:T(8,128)(2,1)} %get-tuple-element.200), channel_id=1, source_target_pairs={{0,2},{2,0},{1,3},{3,1},{4,6},{6,4},{5,7},{7,5},{8,10},{10,8},{9,1... | collective-permute-start | bytes 3981320 | tf_op jit(solution)/shard_map/ppermute | solution.py:106
  643.4 31.5 %collective-permute-start.62 = (bf16[64,2304]{1,0:T(8,128)(2,1)}, bf16[64,2304]{1,0:T(8,128)(2,1)S(1)}, u32[]{:S(2)}, u32[]{:S(2)}) collective-permute-start(bf16[64,2304]{1,0:T(8,128)(2,1)} %get-tuple-element.209), channel_id=1, source_target_pairs={{0,2},{2,0},{1,3},{3,1},{4,6},{6,4},{5,7},{7,5},{8,10},{10,8},{9,1... | collective-permute-start | bytes 884744 | tf_op jit(solution)/shard_map/ppermute | solution.py:106
  645.0 29.9 %collective-permute-start.64 = (bf16[64,2304]{1,0:T(8,128)(2,1)}, bf16[64,2304]{1,0:T(8,128)(2,1)S(1)}, u32[]{:S(2)}, u32[]{:S(2)}) collective-permute-start(bf16[64,2304]{1,0:T(8,128)(2,1)} %get-tuple-element.211), channel_id=1, source_target_pairs={{0,4},{4,0},{1,5},{5,1},{2,6},{6,2},{3,7},{7,3},{8,12},{12,8},{9,1... | collective-permute-start | bytes 884744 | tf_op jit(solution)/shard_map/ppermute | solution.py:106
  649.1 58.0 %all-to-all-start.7 = ((bf16[8,72,1152]{2,1,0:T(8,128)(2,1)}), bf16[8,72,1152]{2,1,0:T(8,128)(2,1)}, u32[]{:S(2)}, u32[]{:S(2)}) async-start(bf16[8,72,1152]{2,1,0:T(8,128)(2,1)} %add_convert_fusion.4), calls=%async_computation.8 | async-start | bytes 2654208 | tf_op jit(solution)/shard_map/all_to_all | solution.py:98
  676.9 19.0 %collective-permute-start.63 = (bf16[128,2304]{1,0:T(8,128)(2,1)S(1)}, bf16[128,2304]{1,0:T(8,128)(2,1)S(1)}, u32[]{:S(2)}, u32[]{:S(2)}) collective-permute-start(bf16[128,2304]{1,0:T(8,128)(2,1)S(1)} %pad_maximum_fusion.10), channel_id=1, source_target_pairs={{0,4},{4,0},{1,5},{5,1},{2,6},{6,2},{3,7},{7,3},{8,12},{12,8},{9,1... | collective-permute-start | bytes 1769480 | tf_op jit(solution)/shard_map/ppermute | solution.py:106
  710.6 20.0 %all-to-all-start.8 = ((bf16[8,72,512]{2,1,0:T(8,128)(2,1)}), bf16[8,72,512]{2,1,0:T(8,128)(2,1)S(1)}, u32[]{:S(2)}, u32[]{:S(2)}) async-start(bf16[8,72,512]{2,1,0:T(8,128)(2,1)} %bitcast.322), calls=%async_computation.9 | async-start | bytes 1179648 | tf_op jit(solution)/shard_map/all_to_all | solution.py:98
  (115 other events, 1146.7 us)
Sparse Core Ops, SparseCore 0:
  44.3 61.9 all-gather.6
  108.8 86.7 all-gather.8
  492.8 44.7 all-gather.10
  611.3 87.8 reduce-scatter.1

commit v2 on v1

--- a/solution.py
+++ b/solution.py
@@ -403,6 +403,7 @@
     others = bf(jnp.pad(others, ((0, 0), (0, 7), (0, 2 * HEAD_DIM - 2 * rows))))
     grad_w = bf(mm_tn(normed_all, grad_qkv))
     grad_qkv, grad_w = hold((grad_qkv, grad_w))
+    grad_halves, _ = hold((grad_halves, grad_attn))
     sums = [
         core_sum(v.reshape(group, 4, rows, ff_own), late)
         for v, late in zip(grad_halves, (grad_head, grad_qkv))
@@ -414,7 +415,7 @@
     grad_w, grad_qkv = hold((grad_w, grad_qkv))
     grad_normed = plane_scatter(bf(mm_nt(grad_qkv, w_own)))
     grad_w = scatter_sum(grad_w, DP)[0]
-    grad_halves = [swap(row_sum(sums[0]), LADDER)]
+    grad_halves = [swap(row_sum(sums[0], grad_qkv), LADDER)]
     grad_halves.append(row_sum(sums[1], grad_halves[0]))
     grad_down_w, grad_halves[1] = hold((sums[2], grad_halves[1]))
     grad_down_w = f32(row_sum(grad_down_w)[0])

time: 752 us -> 744 us (0.989)
  waiting for transfers between devices: 312 us -> 299 us
    ppermute x29, waiting for transfers between devices: 91 us -> 70.5 us  [flip(): return lax.ppermute(v, axis, [(0, 1), (1, 0)])]
    all_to_all x8, waiting for transfers between devices: 45.7 us -> 55.8 us  [swap(): return lax.all_to_all(v, axes, split_axis=0, concat_axis=0, tiled=True)]
    unnamed x194 -> x205, local copies, waits for them, and re-layouts: 22.1 us -> 23.4 us
where the time goes in v2:
time: 744 us; the launch traced here: 734 us
  waiting for transfers between devices  299 us (40%)
  matrix products  118 us (16%)
  starting transfers between devices  100 us (13%)
  local copies, waits for them, and re-layouts  99.8 us (13%)
  other arithmetic  82.3 us (11%)
  between operations  18.6 us (3%)
  blocking collectives  16 us (2%)
    dot_general x21, matrix products, dot(): lax.dot_general(left, right, (dims, ((), ())), preferred_element_type=jnp...  118 us
    ppermute x29, waiting for transfers between devices, flip(): return lax.ppermute(v, axis, [(0, 1), (1, 0)])  70.5 us
    all_to_all x8, waiting for transfers between devices, swap(): return lax.all_to_all(v, axes, split_axis=0, concat_axis=0, tiled=True)  55.8 us
    ppermute x6, waiting for transfers between devices, ring_gather(): ahead = lax.ppermute(ahead, LADDER, back)  40.3 us
    all_to_all x8, starting transfers between devices, swap(): return lax.all_to_all(v, axes, split_axis=0, concat_axis=0, tiled=True)  35.2 us
    ppermute x6, waiting for transfers between devices, ring_scatter(): ahead = lax.ppermute(to_ahead, LADDER, onward)  33.7 us
    convert_element_type x16, other arithmetic, bf(): return v.astype(jnp.bfloat16)  26.3 us
    sub x5, other arithmetic, adam_step(): return (weight - rate * (ratio + decay * weight), first_new, second_new)  24.2 us
  transfers between devices with their start and end apart: 79, of which 44 were waited for; matrix products, arithmetic and copies ran while one was open for 33% of the time, Pallas kernels for 0%

profile of v2, /device:TPU:0, one launch (start us, length us, event | category | flops | bytes accessed | tf_op | source)
XLA Modules:
  0.0 734.3 jit_solution(13285875294684957935)
XLA Ops:
  12.6 16.0 %all_to_all.45 = bf16[8,80,512]{2,1,0:T(8,128)(2,1)} all-to-all(bf16[8,80,512]{2,1,0:T(8,128)(2,1)S(1)} %copy.162), channel_id=1, replica_groups=mesh['dh'=2,'dl'=2,'ctx'=2,'fy'=2,'core'=2] {'ctx','fy','core'}, dimensions={0} | all-to-all | bytes 1310720 | tf_op jit(solution)/shard_map/all_to_all | solution.py:98
  33.3 4.7 collective-permute-done.8
  44.3 7.3 collective-permute-done.12
  53.1 7.1 collective-permute-done.13
  66.0 6.5 copy.164
  80.2 9.4 %collective-permute-done.5 = bf16[128,2304]{1,0:T(8,128)(2,1)S(1)} collective-permute-done((bf16[128,2304]{1,0:T(8,128)(2,1)}, bf16[128,2304]{1,0:T(8,128)(2,1)S(1)}, u32[]{:S(2)}, u32[]{:S(2)}) %collective-permute-start.5) | collective-permute-done | bytes 589856 | tf_op jit(solution)/shard_map/ppermute | solution.py:106
  94.8 11.5 %all-gather.7.cloned.1.call-done = bf16[32,80,512]{2,1,0:T(8,128)(2,1)} async-done(((bf16[8,80,512]{2,1,0:T(8,128)(2,1)}), bf16[32,80,512]{2,1,0:T(8,128)(2,1)}) %all-gather.7.cloned.1.call-update) | async-done | bytes 2621456 | tf_op jit(solution)/shard_map/all_gather | solution.py:294
  133.7 9.4 %all-to-all-done.1 = bf16[8,72,1152]{2,1,0:T(8,128)(2,1)S(1)} async-done(((bf16[8,72,1152]{2,1,0:T(8,128)(2,1)}), bf16[8,72,1152]{2,1,0:T(8,128)(2,1)S(1)}, u32[]{:S(2)}, u32[]{:S(2)}) %all-to-all-start.1) | async-done | bytes 1327136 | tf_op jit(solution)/shard_map/all_to_all | solution.py:98
  150.8 12.0 %all-to-all-done.2 = bf16[8,128,256]{1,2,0:T(8,128)(2,1)S(1)} async-done(((bf16[8,128,256]{1,2,0:T(8,128)(2,1)}), bf16[8,128,256]{1,2,0:T(8,128)(2,1)S(1)}, u32[]{:S(2)}, u32[]{:S(2)}) %all-to-all-start.2) | async-done | bytes 524320 | tf_op jit(solution)/shard_map/all_to_all | solution.py:98
  172.0 4.7 broadcast_in_dim.130
  177.9 17.8 %all-gather.9.cloned.1.call-done = bf16[4,512,2304]{2,1,0:T(8,128)(2,1)} async-done(((bf16[4,64,2304]{2,1,0:T(8,128)(2,1)}), bf16[4,512,2304]{2,1,0:T(8,128)(2,1)}) %all-gather.9.cloned.1.call-update) | async-done | bytes 9437200 | tf_op jit(solution)/shard_map/all_gather | solution.py:304
  195.7 5.2 multiply_reduce_fusion.6
  212.3 8.2 %collective-permute-done.15 = bf16[128,2304]{1,0:T(8,128)(2,1)S(1)} collective-permute-done((bf16[128,2304]{1,0:T(8,128)(2,1)}, bf16[128,2304]{1,0:T(8,128)(2,1)S(1)}, u32[]{:S(2)}, u32[]{:S(2)}) %collective-permute-start.15) | collective-permute-done | bytes 589856 | tf_op jit(solution)/shard_map/ppermute | solution.py:164
  224.7 13.0 %collective-permute-done.16 = bf16[128,2304]{1,0:T(8,128)(2,1)S(1)} collective-permute-done((bf16[128,2304]{1,0:T(8,128)(2,1)S(1)}, bf16[128,2304]{1,0:T(8,128)(2,1)S(1)}, u32[]{:S(2)}, u32[]{:S(2)}) %collective-permute-start.16) | collective-permute-done | bytes 589856 | tf_op jit(solution)/shard_map/ppermute | solution.py:163
  249.3 5.7 collective-permute-done.19
  260.8 6.3 collective-permute-done.20
  270.4 13.5 %fusion.141 = f32[1024,2304]{1,0:T(8,128)S(1)} fusion(bf16[1024,2304]{1,0:T(8,128)(2,1)S(1)} %constant_dynamic-update-slice_fusion, bf16[2304,2304]{1,0:T(8,128)(2,1)} %bitcast.50), kind=kOutput, calls=%fused_computation.353 | convolution fusion | flops 10871635968 | bytes 24772608 | tf_op jit(solution)/shard_map/dot_general | solution.py:38
  287.8 6.5 convolution_convert_fusion.4
  296.8 7.0 collective-permute-done.32
  308.4 12.8 %collective-permute-done.33 = bf16[128,2304]{1,0:T(8,128)(2,1)S(1)} collective-permute-done((bf16[128,2304]{1,0:T(8,128)(2,1)S(1)}, bf16[128,2304]{1,0:T(8,128)(2,1)S(1)}, u32[]{:S(2)}, u32[]{:S(2)}) %collective-permute-start.33) | collective-permute-done | bytes 589856 | tf_op jit(solution)/shard_map/ppermute | solution.py:207
  323.6 11.8 %collective-permute-done.35 = bf16[128,2304]{1,0:T(8,128)(2,1)S(1)} collective-permute-done((bf16[128,2304]{1,0:T(8,128)(2,1)S(1)}, bf16[128,2304]{1,0:T(8,128)(2,1)S(1)}, u32[]{:S(2)}, u32[]{:S(2)}) %collective-permute-start.35) | collective-permute-done | bytes 589856 | tf_op jit(solution)/shard_map/ppermute | solution.py:207
  342.9 12.6 %all-to-all-done.4 = bf16[8,128,256]{1,2,0:T(8,128)(2,1)S(1)} async-done(((bf16[8,128,256]{1,2,0:T(8,128)(2,1)}), bf16[8,128,256]{1,2,0:T(8,128)(2,1)S(1)}, u32[]{:S(2)}, u32[]{:S(2)}) %all-to-all-start.4) | async-done | bytes 524320 | tf_op jit(solution)/shard_map/all_to_all | solution.py:98
  364.0 12.3 %collective-permute-done.40 = bf16[128,2304]{1,0:T(8,128)(2,1)S(1)} collective-permute-done((bf16[128,2304]{1,0:T(8,128)(2,1)S(1)}, bf16[128,2304]{1,0:T(8,128)(2,1)S(1)}, u32[]{:S(2)}, u32[]{:S(2)}) %collective-permute-start.40) | collective-permute-done | bytes 589856 | tf_op jit(solution)/shard_map/ppermute | solution.py:164
  378.4 11.3 %collective-permute-done.42 = bf16[128,2304]{1,0:T(8,128)(2,1)S(1)} collective-permute-done((bf16[128,2304]{1,0:T(8,128)(2,1)S(1)}, bf16[128,2304]{1,0:T(8,128)(2,1)S(1)}, u32[]{:S(2)}, u32[]{:S(2)}) %collective-permute-start.42) | collective-permute-done | bytes 589856 | tf_op jit(solution)/shard_map/ppermute | solution.py:164
  392.0 8.3 %fusion.30 = (bf16[640,1152]{1,0:T(8,128)(2,1)S(1)}, bf16[640,1152]{1,0:T(8,128)(2,1)S(1)}) fusion(f32[1024,2304]{1,0:T(8,128)} %copy-done.7, bf16[640,2304]{1,0:T(8,128)(2,1)S(1)} %constant_dynamic-update-slice_fusion.9, bf16[1152,2304]{1,0:T(8,128)(2,1)S(1)} %bitcast.312), kind=kOutput, calls=%fused_computation.63 | convolution fusion | flops 3415080960 | bytes 17104896 | tf_op jit(solution)/shard_map/dot_general | solution.py:38
  406.3 10.5 %convolution_convert_fusion.5 = bf16[640,2304]{1,0:T(8,128)(2,1)S(1)} fusion(bf16[640,2304]{1,0:T(8,128)(2,1)S(1)} %pad_maximum_fusion, bf16[2304,2304]{1,0:T(8,128)(2,1)} %bitcast.50), kind=kOutput, calls=%fused_computation.26 | convolution fusion | flops 6796247040 | bytes 16515072 | tf_op jit(solution)/shard_map/dot_general | solution.py:38
  418.1 5.9 fusion.43
  424.2 8.3 %convolution_convert_fusion.7 = bf16[384,2304]{1,0:T(8,128)(2,1)S(1)} fusion(bf16[384,2304]{1,0:T(8,128)(2,1)S(1)} %pad_maximum_fusion.2, bf16[2304,2304]{1,0:T(8,128)(2,1)} %bitcast.50), kind=kOutput, calls=%fused_computation.44 | convolution fusion | flops 4077748224 | bytes 14155776 | tf_op jit(solution)/shard_map/dot_general | solution.py:38
  435.2 4.4 collective-permute-done.48
  439.6 4.6 collective-permute-done.47
  446.5 8.0 %convolution_convert_fusion.1 = bf16[2304,1152]{1,0:T(8,128)(2,1)} fusion(bf16[1024,2304]{1,0:T(8,128)(2,1)S(1)} %bitcast.339, bf16[1024,2304]{1,0:T(8,128)(2,1)S(1)} %constant_dynamic-update-slice_fusion.18), kind=kOutput, calls=%fused_computation.1 | convolution fusion | flops 5438472192 | bytes 12386304 | tf_op jit(solution)/shard_map/dot_general | solution.py:38
  461.3 8.0 %convolution_convert_fusion.2 = bf16[2304,1152]{1,0:T(8,128)(2,1)} fusion(bf16[1024,2304]{1,0:T(8,128)(2,1)S(1)} %bitcast.339, bf16[1024,2304]{1,0:T(8,128)(2,1)S(1)} %constant_dynamic-update-slice_fusion.18), kind=kOutput, calls=%fused_computation.2 | convolution fusion | flops 5438472192 | bytes 12386304 | tf_op jit(solution)/shard_map/dot_general | solution.py:38
  469.4 5.1 collective-permute-done.51
  479.5 7.5 %convolution_convert_fusion = bf16[1152,2304]{1,0:T(8,128)(2,1)} fusion(bf16[1024,1152]{1,0:T(8,128)(2,1)S(1)} %copy-done.27, bf16[384,2304]{1,0:T(8,128)(2,1)S(1)} %copy-done.50, bf16[640,2304]{1,0:T(8,128)(2,1)S(1)} %copy-done.56), kind=kOutput, calls=%fused_computation | convolution fusion | flops 5447909376 | bytes 12386304 | tf_op jit(solution)/shard_map/dot_general | solution.py:38
  492.7 6.8 convolution_convert_fusion.9
  504.6 5.5 dynamic-slice_bitcast_fusion
  540.5 5.3 convolution_convert_fusion.8
  545.8 6.2 convolution_convert_fusion.6
  559.2 4.7 convolution_convert_fusion.3
  572.3 5.8 all-to-all-start.6
  587.5 26.4 %collective-permute-done.58 = bf16[8,72,1152]{2,1,0:T(8,128)(2,1)} collective-permute-done((bf16[8,72,1152]{2,1,0:T(8,128)(2,1)}, bf16[8,72,1152]{2,1,0:T(8,128)(2,1)}, u32[]{:S(2)}, u32[]{:S(2)}) %collective-permute-start.58) | collective-permute-done | bytes 1327136 | tf_op jit(solution)/shard_map/ppermute | solution.py:106
  613.9 18.1 %all-to-all-done.6 = bf16[8,72,1152]{2,1,0:T(8,128)(2,1)} async-done(((bf16[8,72,1152]{2,1,0:T(8,128)(2,1)}), bf16[8,72,1152]{2,1,0:T(8,128)(2,1)}, u32[]{:S(2)}, u32[]{:S(2)}) %all-to-all-start.6) | async-done | bytes 1327136 | tf_op jit(solution)/shard_map/all_to_all | solution.py:98
  635.3 5.2 collective-permute-start.64
  654.4 4.3 all-to-all-start.7
  668.9 14.4 %collective-permute-done.66 = bf16[1,288,2304]{2,1,0:T(8,128)(2,1)} collective-permute-done((bf16[1,288,2304]{2,1,0:T(8,128)(2,1)}, bf16[1,288,2304]{2,1,0:T(8,128)(2,1)}, u32[]{:S(2)}, u32[]{:S(2)}) %collective-permute-start.66) | collective-permute-done | bytes 1327136 | tf_op jit(solution)/shard_map/ppermute | solution.py:106
  683.3 7.0 convert_subtract_fusion.1
  699.2 6.2 all-to-all-start.8
  707.7 12.5 %convert_subtract_fusion = (f32[72,18432]{1,0:T(8,128)}, f32[72,18432]{1,0:T(8,128)}, f32[72,18432]{1,0:T(8,128)}, f32[72]{0:T(128)S(1)}) fusion(bf16[72,18432]{1,0:T(8,128)(2,1)S(1)} %copy-done.6, bf16[72,9216]{1,0:T(8,128)(2,1)} %bitcast.301, bf16[72,9216]{1,0:T(8,128)(2,1)S(1)} %bitcast.300, f32[72,18432]{1,0:T(8,128)} %param.30, f32[72,18432]{1,0:T(8,128)} %param.31), kind=kLoop, calls=%fused_computation.11 | loop fusion | flops 29196216 | bytes 31850784 | tf_op jit(solution)/shard_map/sub | solution.py:86
  (503 shorter events, 283.9 us)
Async XLA Ops:
  7.2 99.1 %all-gather.7.cloned.1.call-start = ((), (), s32[]{:S(2)}) async-start(), calls=%async_computation.11 | async-start | bytes 3276800 | tf_op jit(solution)/shard_map/all_gather | solution.py:294
  44.2 151.5 %all-gather.9.cloned.1.call-start = ((), (), s32[]{:S(2)}) async-start(), calls=%async_computation.12 | async-start | bytes 10616832 | tf_op jit(solution)/shard_map/all_gather | solution.py:304
  63.7 13.7 %collective-permute-start.3 = (bf16[128,2304]{1,0:T(8,128)(2,1)S(1)}, bf16[128,2304]{1,0:T(8,128)(2,1)S(1)}, u32[]{:S(2)}, u32[]{:S(2)}) collective-permute-start(bf16[128,2304]{1,0:T(8,128)(2,1)S(1)} %bitcast.292), channel_id=1, source_target_pairs={{0,4},{4,0},{1,5},{5,1},{2,6},{6,2},{3,7},{7,3},{8,12},{12,8},{9,1... | collective-permute-start | bytes 1769480 | tf_op jit(solution)/shard_map/ppermute | solution.py:106
  107.5 35.6 %all-to-all-start.1 = ((bf16[8,72,1152]{2,1,0:T(8,128)(2,1)}), bf16[8,72,1152]{2,1,0:T(8,128)(2,1)S(1)}, u32[]{:S(2)}, u32[]{:S(2)}) async-start(bf16[8,72,1152]{2,1,0:T(8,128)(2,1)} %copy.163), calls=%async_computation.1 | async-start | bytes 2654208 | tf_op jit(solution)/shard_map/all_to_all | solution.py:98
  144.4 18.4 %all-to-all-start.2 = ((bf16[8,128,256]{1,2,0:T(8,128)(2,1)}), bf16[8,128,256]{1,2,0:T(8,128)(2,1)S(1)}, u32[]{:S(2)}, u32[]{:S(2)}) async-start(bf16[8,128,256]{1,2,0:T(8,128)(2,1)} %copy_bitcast_fusion.2), calls=%async_computation.2 | async-start | bytes 1048576 | tf_op jit(solution)/shard_map/all_to_all | solution.py:98
  162.8 46.4 %collective-permute-start.23 = (bf16[8,72,1152]{2,1,0:T(8,128)(2,1)}, bf16[8,72,1152]{2,1,0:T(8,128)(2,1)}, u32[]{:S(2)}, u32[]{:S(2)}) collective-permute-start(bf16[8,72,1152]{2,1,0:T(8,128)(2,1)} %copy-done.16), channel_id=1, source_target_pairs={{0,2},{2,0},{1,3},{3,1},{4,6},{6,4},{5,7},{7,5},{8,10},{10,8},{9,1... | collective-permute-start | bytes 3981320 | tf_op jit(solution)/shard_map/ppermute | solution.py:106
  164.3 42.3 %collective-permute-start.22 = (bf16[8,72,1152]{2,1,0:T(8,128)(2,1)}, bf16[8,72,1152]{2,1,0:T(8,128)(2,1)}, u32[]{:S(2)}, u32[]{:S(2)}) collective-permute-start(bf16[8,72,1152]{2,1,0:T(8,128)(2,1)} %copy-done.16), channel_id=1, source_target_pairs={{0,1},{1,0},{2,3},{3,2},{4,5},{5,4},{6,7},{7,6},{8,9},{9,8},{10,11... | collective-permute-start | bytes 3981320 | tf_op jit(solution)/shard_map/ppermute | solution.py:106
  166.9 42.3 %all-to-all-start.3 = ((bf16[8,72,1152]{2,1,0:T(8,128)(2,1)}), bf16[8,72,1152]{2,1,0:T(8,128)(2,1)}, u32[]{:S(2)}, u32[]{:S(2)}) async-start(bf16[8,72,1152]{2,1,0:T(8,128)(2,1)} %copy.168), calls=%async_computation.3 | async-start | bytes 2654208 | tf_op jit(solution)/shard_map/all_to_all | solution.py:98
  202.7 17.8 %collective-permute-start.15 = (bf16[128,2304]{1,0:T(8,128)(2,1)}, bf16[128,2304]{1,0:T(8,128)(2,1)S(1)}, u32[]{:S(2)}, u32[]{:S(2)}) collective-permute-start(bf16[128,2304]{1,0:T(8,128)(2,1)} %get-tuple-element.174), channel_id=1, source_target_pairs={{8,0},{16,8},{24,16},{28,24},{20,28},{12,20},{4,12},{0,4},{9,1},{1... | collective-permute-start | bytes 1769480 | tf_op jit(solution)/shard_map/ppermute | solution.py:164
  205.3 17.5 %collective-permute-start.14 = (bf16[128,2304]{1,0:T(8,128)(2,1)}, bf16[128,2304]{1,0:T(8,128)(2,1)S(1)}, u32[]{:S(2)}, u32[]{:S(2)}) collective-permute-start(bf16[128,2304]{1,0:T(8,128)(2,1)} %get-tuple-element.174), channel_id=1, source_target_pairs={{0,8},{8,16},{16,24},{24,28},{28,20},{20,12},{12,4},{4,0},{1,9},{9... | collective-permute-start | bytes 1769480 | tf_op jit(solution)/shard_map/ppermute | solution.py:163
  209.2 37.4 %collective-permute-start.26 = (bf16[8,72,1152]{2,1,0:T(8,128)(2,1)}, bf16[8,72,1152]{2,1,0:T(8,128)(2,1)S(1)}, u32[]{:S(2)}, u32[]{:S(2)}) collective-permute-start(bf16[8,72,1152]{2,1,0:T(8,128)(2,1)} %all-to-all-done.3), channel_id=1, source_target_pairs={{0,2},{2,0},{1,3},{3,1},{4,6},{6,4},{5,7},{7,5},{8,10},{10,8},{9,1... | collective-permute-start | bytes 3981320 | tf_op jit(solution)/shard_map/ppermute | solution.py:106
  209.2 37.6 %collective-permute-start.25 = (bf16[8,72,1152]{2,1,0:T(8,128)(2,1)}, bf16[8,72,1152]{2,1,0:T(8,128)(2,1)S(1)}, u32[]{:S(2)}, u32[]{:S(2)}) collective-permute-start(bf16[8,72,1152]{2,1,0:T(8,128)(2,1)} %all-to-all-done.3), channel_id=1, source_target_pairs={{0,1},{1,0},{2,3},{3,2},{4,5},{5,4},{6,7},{7,6},{8,9},{9,8},{10,11... | collective-permute-start | bytes 3981320 | tf_op jit(solution)/shard_map/ppermute | solution.py:106
  209.3 31.6 %collective-permute-start.24 = (bf16[8,72,1152]{2,1,0:T(8,128)(2,1)}, bf16[8,72,1152]{2,1,0:T(8,128)(2,1)S(1)}, u32[]{:S(2)}, u32[]{:S(2)}) collective-permute-start(bf16[8,72,1152]{2,1,0:T(8,128)(2,1)} %collective-permute-done.23), channel_id=1, source_target_pairs={{0,1},{1,0},{2,3},{3,2},{4,5},{5,4},{6,7},{7,6},{8,9},{9,8},{10,11... | collective-permute-start | bytes 3981320 | tf_op jit(solution)/shard_map/ppermute | solution.py:106
  220.5 18.5 %collective-permute-start.17 = (bf16[128,2304]{1,0:T(8,128)(2,1)S(1)}, bf16[128,2304]{1,0:T(8,128)(2,1)S(1)}, u32[]{:S(2)}, u32[]{:S(2)}) collective-permute-start(bf16[128,2304]{1,0:T(8,128)(2,1)S(1)} %collective-permute-done.15), channel_id=1, source_target_pairs={{8,0},{16,8},{24,16},{28,24},{20,28},{12,20},{4,12},{0,4},{9,1},{1... | collective-permute-start | bytes 1769480 | tf_op jit(solution)/shard_map/ppermute | solution.py:164
  222.8 14.9 %collective-permute-start.16 = (bf16[128,2304]{1,0:T(8,128)(2,1)S(1)}, bf16[128,2304]{1,0:T(8,128)(2,1)S(1)}, u32[]{:S(2)}, u32[]{:S(2)}) collective-permute-start(bf16[128,2304]{1,0:T(8,128)(2,1)S(1)} %collective-permute-done.14), channel_id=1, source_target_pairs={{0,8},{8,16},{16,24},{24,28},{28,20},{20,12},{12,4},{4,0},{1,9},{9... | collective-permute-start | bytes 1769480 | tf_op jit(solution)/shard_map/ppermute | solution.py:163
  237.7 31.2 %collective-permute-start.29 = (bf16[1,288,2304]{2,1,0:T(8,128)(2,1)S(1)}, bf16[1,288,2304]{2,1,0:T(8,128)(2,1)S(1)}, u32[]{:S(2)}, u32[]{:S(2)}) collective-permute-start(bf16[1,288,2304]{2,1,0:T(8,128)(2,1)S(1)} %bitcast.298), channel_id=1, source_target_pairs={{0,2},{2,0},{1,3},{3,1},{4,6},{6,4},{5,7},{7,5},{8,10},{10,8},{9,1... | collective-permute-start | bytes 3981320 | tf_op jit(solution)/shard_map/ppermute | solution.py:106
  239.0 29.9 %collective-permute-start.28 = (bf16[1,288,2304]{2,1,0:T(8,128)(2,1)S(1)}, bf16[1,288,2304]{2,1,0:T(8,128)(2,1)S(1)}, u32[]{:S(2)}, u32[]{:S(2)}) collective-permute-start(bf16[1,288,2304]{2,1,0:T(8,128)(2,1)S(1)} %bitcast.299), channel_id=1, source_target_pairs={{0,1},{1,0},{2,3},{3,2},{4,5},{5,4},{6,7},{7,6},{8,9},{9,8},{10,11... | collective-permute-start | bytes 3981320 | tf_op jit(solution)/shard_map/ppermute | solution.py:106
  240.9 14.0 %collective-permute-start.19 = (bf16[128,2304]{1,0:T(8,128)(2,1)S(1)}, bf16[128,2304]{1,0:T(8,128)(2,1)S(1)}, u32[]{:S(2)}, u32[]{:S(2)}) collective-permute-start(bf16[128,2304]{1,0:T(8,128)(2,1)S(1)} %collective-permute-done.17), channel_id=1, source_target_pairs={{8,0},{16,8},{24,16},{28,24},{20,28},{12,20},{4,12},{0,4},{9,1},{1... | collective-permute-start | bytes 1769480 | tf_op jit(solution)/shard_map/ppermute | solution.py:164
  246.6 13.8 %collective-permute-start.18 = (bf16[128,2304]{1,0:T(8,128)(2,1)S(1)}, bf16[128,2304]{1,0:T(8,128)(2,1)S(1)}, u32[]{:S(2)}, u32[]{:S(2)}) collective-permute-start(bf16[128,2304]{1,0:T(8,128)(2,1)S(1)} %collective-permute-done.16), channel_id=1, source_target_pairs={{0,8},{8,16},{16,24},{24,28},{28,20},{20,12},{12,4},{4,0},{1,9},{9... | collective-permute-start | bytes 1769480 | tf_op jit(solution)/shard_map/ppermute | solution.py:163
  246.8 22.4 %collective-permute-start.27 = (bf16[8,72,1152]{2,1,0:T(8,128)(2,1)S(1)}, bf16[8,72,1152]{2,1,0:T(8,128)(2,1)S(1)}, u32[]{:S(2)}, u32[]{:S(2)}) collective-permute-start(bf16[8,72,1152]{2,1,0:T(8,128)(2,1)S(1)} %collective-permute-done.26), channel_id=1, source_target_pairs={{0,1},{1,0},{2,3},{3,2},{4,5},{5,4},{6,7},{7,6},{8,9},{9,8},{10,11... | collective-permute-start | bytes 3981320 | tf_op jit(solution)/shard_map/ppermute | solution.py:106
  268.9 18.7 %collective-permute-start.30 = (bf16[1,288,2304]{2,1,0:T(8,128)(2,1)S(1)}, bf16[1,288,2304]{2,1,0:T(8,128)(2,1)S(1)}, u32[]{:S(2)}, u32[]{:S(2)}) collective-permute-start(bf16[1,288,2304]{2,1,0:T(8,128)(2,1)S(1)} %collective-permute-done.29), channel_id=1, source_target_pairs={{0,1},{1,0},{2,3},{3,2},{4,5},{5,4},{6,7},{7,6},{8,9},{9,8},{10,11... | collective-permute-start | bytes 3981320 | tf_op jit(solution)/shard_map/ppermute | solution.py:106
  306.3 14.9 %collective-permute-start.33 = (bf16[128,2304]{1,0:T(8,128)(2,1)S(1)}, bf16[128,2304]{1,0:T(8,128)(2,1)S(1)}, u32[]{:S(2)}, u32[]{:S(2)}) collective-permute-start(bf16[128,2304]{1,0:T(8,128)(2,1)S(1)} %get-tuple-element.94), channel_id=1, source_target_pairs={{0,8},{8,16},{16,24},{24,28},{28,20},{20,12},{12,4},{4,0},{1,9},{9... | collective-permute-start | bytes 1769480 | tf_op jit(solution)/shard_map/ppermute | solution.py:207
  306.5 14.7 %collective-permute-start.34 = (bf16[128,2304]{1,0:T(8,128)(2,1)S(1)}, bf16[128,2304]{1,0:T(8,128)(2,1)S(1)}, u32[]{:S(2)}, u32[]{:S(2)}) collective-permute-start(bf16[128,2304]{1,0:T(8,128)(2,1)S(1)} %get-tuple-element.95), channel_id=1, source_target_pairs={{8,0},{16,8},{24,16},{28,24},{20,28},{12,20},{4,12},{0,4},{9,1},{1... | collective-permute-start | bytes 1769480 | tf_op jit(solution)/shard_map/ppermute | solution.py:208
  321.6 13.9 %collective-permute-start.35 = (bf16[128,2304]{1,0:T(8,128)(2,1)S(1)}, bf16[128,2304]{1,0:T(8,128)(2,1)S(1)}, u32[]{:S(2)}, u32[]{:S(2)}) collective-permute-start(bf16[128,2304]{1,0:T(8,128)(2,1)S(1)} %get-tuple-element.96), channel_id=1, source_target_pairs={{0,8},{8,16},{16,24},{24,28},{28,20},{20,12},{12,4},{4,0},{1,9},{9... | collective-permute-start | bytes 1769480 | tf_op jit(solution)/shard_map/ppermute | solution.py:207
  337.2 20.5 %collective-permute-start.37 = (bf16[128,2304]{1,0:T(8,128)(2,1)}, bf16[128,2304]{1,0:T(8,128)(2,1)}, u32[]{:S(2)}, u32[]{:S(2)}) collective-permute-start(bf16[128,2304]{1,0:T(8,128)(2,1)} %get-tuple-element.98), channel_id=1, source_target_pairs={{0,8},{8,16},{16,24},{24,28},{28,20},{20,12},{12,4},{4,0},{1,9},{9... | collective-permute-start | bytes 1769480 | tf_op jit(solution)/shard_map/ppermute | solution.py:207
  338.8 18.9 %collective-permute-start.38 = (bf16[128,2304]{1,0:T(8,128)(2,1)}, bf16[128,2304]{1,0:T(8,128)(2,1)}, u32[]{:S(2)}, u32[]{:S(2)}) collective-permute-start(bf16[128,2304]{1,0:T(8,128)(2,1)} %get-tuple-element.99), channel_id=1, source_target_pairs={{8,0},{16,8},{24,16},{28,24},{20,28},{12,20},{4,12},{0,4},{9,1},{1... | collective-permute-start | bytes 1769480 | tf_op jit(solution)/shard_map/ppermute | solution.py:208
  339.2 16.3 %all-to-all-start.4 = ((bf16[8,128,256]{1,2,0:T(8,128)(2,1)}), bf16[8,128,256]{1,2,0:T(8,128)(2,1)S(1)}, u32[]{:S(2)}, u32[]{:S(2)}) async-start(bf16[8,128,256]{1,2,0:T(8,128)(2,1)} %bitcast.38), calls=%async_computation.4 | async-start | bytes 1048576 | tf_op jit(solution)/shard_map/all_to_all | solution.py:98
  342.7 196.6 %all-gather.11.cloned.1.call-start = ((), (), s32[]{:S(2)}) async-start(), calls=%async_computation.13 | async-start | bytes 5971968 | tf_op jit(solution)/shard_map/all_gather | solution.py:397
  361.5 14.8 %collective-permute-start.40 = (bf16[128,2304]{1,0:T(8,128)(2,1)S(1)}, bf16[128,2304]{1,0:T(8,128)(2,1)S(1)}, u32[]{:S(2)}, u32[]{:S(2)}) collective-permute-start(bf16[128,2304]{1,0:T(8,128)(2,1)S(1)} %get-tuple-element.172), channel_id=1, source_target_pairs={{8,0},{16,8},{24,16},{28,24},{20,28},{12,20},{4,12},{0,4},{9,1},{1... | collective-permute-start | bytes 1769480 | tf_op jit(solution)/shard_map/ppermute | solution.py:164
  363.7 14.4 %collective-permute-start.39 = (bf16[128,2304]{1,0:T(8,128)(2,1)S(1)}, bf16[128,2304]{1,0:T(8,128)(2,1)S(1)}, u32[]{:S(2)}, u32[]{:S(2)}) collective-permute-start(bf16[128,2304]{1,0:T(8,128)(2,1)S(1)} %get-tuple-element.172), channel_id=1, source_target_pairs={{0,8},{8,16},{16,24},{24,28},{28,20},{20,12},{12,4},{4,0},{1,9},{9... | collective-permute-start | bytes 1769480 | tf_op jit(solution)/shard_map/ppermute | solution.py:163
  403.3 14.7 %collective-permute-start.46 = (bf16[64,2304]{1,0:T(8,128)(2,1)S(1)}, bf16[64,2304]{1,0:T(8,128)(2,1)S(1)}, u32[]{:S(2)}, u32[]{:S(2)}) collective-permute-start(bf16[64,2304]{1,0:T(8,128)(2,1)S(1)} %slice.392), channel_id=1, source_target_pairs={{8,0},{16,8},{24,16},{28,24},{20,28},{12,20},{4,12},{0,4},{9,1},{1... | collective-permute-start | bytes 884744 | tf_op jit(solution)/shard_map/ppermute | solution.py:169
  444.4 14.1 %collective-permute-start.49 = (bf16[128,2304]{1,0:T(8,128)(2,1)S(1)}, bf16[128,2304]{1,0:T(8,128)(2,1)S(1)}, u32[]{:S(2)}, u32[]{:S(2)}) collective-permute-start(bf16[128,2304]{1,0:T(8,128)(2,1)S(1)} %pad_maximum_fusion.8), channel_id=1, source_target_pairs={{0,8},{8,16},{16,24},{24,28},{28,20},{20,12},{12,4},{4,0},{1,9},{9... | collective-permute-start | bytes 1769480 | tf_op jit(solution)/shard_map/ppermute | solution.py:207
  444.5 14.1 %collective-permute-start.50 = (bf16[128,2304]{1,0:T(8,128)(2,1)S(1)}, bf16[128,2304]{1,0:T(8,128)(2,1)S(1)}, u32[]{:S(2)}, u32[]{:S(2)}) collective-permute-start(bf16[128,2304]{1,0:T(8,128)(2,1)S(1)} %pad_maximum_fusion.9), channel_id=1, source_target_pairs={{8,0},{16,8},{24,16},{28,24},{20,28},{12,20},{4,12},{0,4},{9,1},{1... | collective-permute-start | bytes 1769480 | tf_op jit(solution)/shard_map/ppermute | solution.py:208
  458.9 15.6 %collective-permute-start.51 = (bf16[128,2304]{1,0:T(8,128)(2,1)S(1)}, bf16[128,2304]{1,0:T(8,128)(2,1)S(1)}, u32[]{:S(2)}, u32[]{:S(2)}) collective-permute-start(bf16[128,2304]{1,0:T(8,128)(2,1)S(1)} %get-tuple-element.108), channel_id=1, source_target_pairs={{0,8},{8,16},{16,24},{24,28},{28,20},{20,12},{12,4},{4,0},{1,9},{9... | collective-permute-start | bytes 1769480 | tf_op jit(solution)/shard_map/ppermute | solution.py:207
  461.0 15.7 %collective-permute-start.52 = (bf16[128,2304]{1,0:T(8,128)(2,1)S(1)}, bf16[128,2304]{1,0:T(8,128)(2,1)S(1)}, u32[]{:S(2)}, u32[]{:S(2)}) collective-permute-start(bf16[128,2304]{1,0:T(8,128)(2,1)S(1)} %get-tuple-element.109), channel_id=1, source_target_pairs={{8,0},{16,8},{24,16},{28,24},{20,28},{12,20},{4,12},{0,4},{9,1},{1... | collective-permute-start | bytes 1769480 | tf_op jit(solution)/shard_map/ppermute | solution.py:208
  510.0 23.6 %collective-permute-start.59 = (bf16[8,2,72,1152]{3,2,1,0:T(8,128)(2,1)}, bf16[8,2,72,1152]{3,2,1,0:T(8,128)(2,1)}, u32[]{:S(2)}, u32[]{:S(2)}) collective-permute-start(bf16[8,2,72,1152]{3,2,1,0:T(8,128)(2,1)} %get-tuple-element.182), channel_id=1, source_target_pairs={{0,1},{1,0},{2,3},{3,2},{4,5},{5,4},{6,7},{7,6},{8,9},{9,8},{10,11... | collective-permute-start | bytes 7962632 | tf_op jit(solution)/shard_map/ppermute | solution.py:106
  523.4 60.2 %collective-permute-start.56 = (bf16[1,2,288,2304]{3,2,1,0:T(8,128)(2,1)}, bf16[1,2,288,2304]{3,2,1,0:T(8,128)(2,1)}, u32[]{:S(2)}, u32[]{:S(2)}) collective-permute-start(bf16[1,2,288,2304]{3,2,1,0:T(8,128)(2,1)} %get-tuple-element.186), channel_id=1, source_target_pairs={{0,1},{1,0},{2,3},{3,2},{4,5},{5,4},{6,7},{7,6},{8,9},{9,8},{10,11... | collective-permute-start | bytes 7962632 | tf_op jit(solution)/shard_map/ppermute | solution.py:106
  526.6 41.2 %collective-permute-start.57 = (bf16[8,2,72,1152]{3,2,1,0:T(8,128)(2,1)}, bf16[8,2,72,1152]{3,2,1,0:T(8,128)(2,1)}, u32[]{:S(2)}, u32[]{:S(2)}) collective-permute-start(bf16[8,2,72,1152]{3,2,1,0:T(8,128)(2,1)} %get-tuple-element.184), channel_id=1, source_target_pairs={{0,1},{1,0},{2,3},{3,2},{4,5},{5,4},{6,7},{7,6},{8,9},{9,8},{10,11... | collective-permute-start | bytes 7962632 | tf_op jit(solution)/shard_map/ppermute | solution.py:106
  537.8 31.8 %collective-permute-start.60 = (bf16[8,72,1152]{2,1,0:T(8,128)(2,1)}, bf16[8,72,1152]{2,1,0:T(8,128)(2,1)}, u32[]{:S(2)}, u32[]{:S(2)}) collective-permute-start(bf16[8,72,1152]{2,1,0:T(8,128)(2,1)} %get-tuple-element.206), channel_id=1, source_target_pairs={{0,2},{2,0},{1,3},{3,1},{4,6},{6,4},{5,7},{7,5},{8,10},{10,8},{9,1... | collective-permute-start | bytes 3981320 | tf_op jit(solution)/shard_map/ppermute | solution.py:106
  567.6 64.4 %collective-permute-start.61 = (bf16[4,128,2304]{2,1,0:T(8,128)(2,1)}, bf16[4,128,2304]{2,1,0:T(8,128)(2,1)}, u32[]{:S(2)}, u32[]{:S(2)}) collective-permute-start(bf16[4,128,2304]{2,1,0:T(8,128)(2,1)} %dynamic-slice_bitcast_fusion.6), channel_id=1, source_target_pairs={{0,1},{1,0},{2,3},{3,2},{4,5},{5,4},{6,7},{7,6},{8,9},{9,8},{10,11... | collective-permute-start | bytes 7077896 | tf_op jit(solution)/shard_map/ppermute | solution.py:106
  572.3 59.7 %all-to-all-start.6 = ((bf16[8,72,1152]{2,1,0:T(8,128)(2,1)}), bf16[8,72,1152]{2,1,0:T(8,128)(2,1)}, u32[]{:S(2)}, u32[]{:S(2)}) async-start(bf16[8,72,1152]{2,1,0:T(8,128)(2,1)} %add_convert_fusion.5), calls=%async_computation.7 | async-start | bytes 2654208 | tf_op jit(solution)/shard_map/all_to_all | solution.py:98
  578.1 112.2 %reduce-scatter.2.cloned.1.call-start = ((), (), s32[]{:S(2)}) async-start(), calls=%async_computation.10 | async-start | bytes 4464640 | tf_op jit(solution)/shard_map/reduce_scatter | solution.py:94
  583.1 30.8 %collective-permute-start.58 = (bf16[8,72,1152]{2,1,0:T(8,128)(2,1)}, bf16[8,72,1152]{2,1,0:T(8,128)(2,1)}, u32[]{:S(2)}, u32[]{:S(2)}) collective-permute-start(bf16[8,72,1152]{2,1,0:T(8,128)(2,1)} %get-tuple-element.208), channel_id=1, source_target_pairs={{0,2},{2,0},{1,3},{3,1},{4,6},{6,4},{5,7},{7,5},{8,10},{10,8},{9,1... | collective-permute-start | bytes 3981320 | tf_op jit(solution)/shard_map/ppermute | solution.py:106
  646.9 18.0 %collective-permute-start.65 = (bf16[128,2304]{1,0:T(8,128)(2,1)S(1)}, bf16[128,2304]{1,0:T(8,128)(2,1)}, u32[]{:S(2)}, u32[]{:S(2)}) collective-permute-start(bf16[128,2304]{1,0:T(8,128)(2,1)S(1)} %pad_maximum_fusion.11), channel_id=1, source_target_pairs={{0,2},{2,0},{1,3},{3,1},{4,6},{6,4},{5,7},{7,5},{8,10},{10,8},{9,1... | collective-permute-start | bytes 1769480 | tf_op jit(solution)/shard_map/ppermute | solution.py:106
  650.6 16.9 %collective-permute-start.63 = (bf16[128,2304]{1,0:T(8,128)(2,1)S(1)}, bf16[128,2304]{1,0:T(8,128)(2,1)}, u32[]{:S(2)}, u32[]{:S(2)}) collective-permute-start(bf16[128,2304]{1,0:T(8,128)(2,1)S(1)} %pad_maximum_fusion.10), channel_id=1, source_target_pairs={{0,4},{4,0},{1,5},{5,1},{2,6},{6,2},{3,7},{7,3},{8,12},{12,8},{9,1... | collective-permute-start | bytes 1769480 | tf_op jit(solution)/shard_map/ppermute | solution.py:106
  654.4 28.9 %collective-permute-start.66 = (bf16[1,288,2304]{2,1,0:T(8,128)(2,1)}, bf16[1,288,2304]{2,1,0:T(8,128)(2,1)}, u32[]{:S(2)}, u32[]{:S(2)}) collective-permute-start(bf16[1,288,2304]{2,1,0:T(8,128)(2,1)} %get-tuple-element.204), channel_id=1, source_target_pairs={{0,2},{2,0},{1,3},{3,1},{4,6},{6,4},{5,7},{7,5},{8,10},{10,8},{9,1... | collective-permute-start | bytes 3981320 | tf_op jit(solution)/shard_map/ppermute | solution.py:106
  654.4 41.3 %all-to-all-start.7 = ((bf16[8,72,1152]{2,1,0:T(8,128)(2,1)}), bf16[8,72,1152]{2,1,0:T(8,128)(2,1)}, u32[]{:S(2)}, u32[]{:S(2)}) async-start(bf16[8,72,1152]{2,1,0:T(8,128)(2,1)} %add_convert_fusion.4), calls=%async_computation.8 | async-start | bytes 2654208 | tf_op jit(solution)/shard_map/all_to_all | solution.py:98
  699.2 22.6 %all-to-all-start.8 = ((bf16[8,72,512]{2,1,0:T(8,128)(2,1)}), bf16[8,72,512]{2,1,0:T(8,128)(2,1)S(1)}, u32[]{:S(2)}, u32[]{:S(2)}) async-start(bf16[8,72,512]{2,1,0:T(8,128)(2,1)} %bitcast.324), calls=%async_computation.9 | async-start | bytes 1179648 | tf_op jit(solution)/shard_map/all_to_all | solution.py:98
  (120 other events, 1158.8 us)
Sparse Core Ops, SparseCore 0:
  44.3 61.9 all-gather.6
  108.8 86.8 all-gather.8
  492.8 44.7 all-gather.10
  583.8 80.1 reduce-scatter.1
